TPU v7x, 256 devices: a whole 4x4x8 slice. The times are simulated.
256 devices in a mesh: prompt: 8 (over z_hi, y), group: 8 (over x, core), tensor: 4 (over z_lo).
Axes of the slice: x: 4, y: 4, z: 8 (z_hi: 2, z_lo: 4; z = z_hi * 4 + z_lo), core: 2. Of those that a mesh axis runs over, the one named last changes fastest.
Arguments:
- query: bfloat16 [64, 256, 5120], P(('prompt', 'group'), None, 'tensor'), may hold values from -33 to 33
- own_kv: bfloat16 [64, 256, 2, 1024], P(('prompt', 'group'), None, None, 'tensor'), may hold values from -6 to 6
- prompt_kv: bfloat16 [8, 2048, 2, 1024], P('group', ('prompt', 'tensor')), may hold values from -14 to 14
- d_out: bfloat16 [64, 256, 5120], P(('prompt', 'group'), None, 'tensor'), may hold values from -6 to 6
- prompt_of: int32 [8], replicated, may hold values from 0 to 7, as said below
- comp_len: int32 [64], P(('prompt', 'group')), may hold values from 1 to 256, 10240 in all
Outputs:
- attn_out: bfloat16 [64, 256, 5120], P(('prompt', 'group'), None, 'tensor')
- d_query: bfloat16 [64, 256, 5120], P(('prompt', 'group'), None, 'tensor')
- d_own_kv: bfloat16 [64, 256, 2, 1024], P(('prompt', 'group'), None, None, 'tensor')
- d_prompt_kv: bfloat16 [8, 2048, 2, 1024], P('group', ('prompt', 'tensor'))
Inputs may be any that keep to these rules, and one draw needn't show every extreme that they name: `prompt_of`: a permutation: every prompt belongs to exactly one index of group. `comp_len`: some sample has all 256 tokens live.
All inputs are finite; a program needn't handle non-finite values. No bound on the sum of `comp_len` on one device may be relied on, other than what follows from the above.
Results may differ from a plain program's by a relative error of at most 0.035.
Values may be sent and summed in bfloat16 or wider, within the bound.
No kernel may reach another device: no remote copies, remote signals or barrier semaphores. Data moves between devices by JAX's collectives and lax.ppermute only.
A program may use at most 128 MiB of HBM per device.

v0:
```python
import math
import jax
import jax.numpy as jnp
from jax import lax
from jax.experimental import pallas as pl
from jax.experimental.pallas import tpu as pltpu
from jax.sharding import Mesh, PartitionSpec as P

HEADS = 40
KV_HEADS = 8
HEAD = 128
RATIO = HEADS // KV_HEADS
ROWS = 256
SEG = 512
TILE = 256
SCALE = HEAD ** (-0.5)
LOG2 = SCALE * math.log2(math.e)
VMEM_LIMIT = 60 * 1024 * 1024

F32 = jnp.float32
BF16 = jnp.bfloat16


def dot_nt(a, b):
    return lax.dot_general(a, b, (((1,), (1,)), ((), ())), preferred_element_type=F32)


def dot_nn(a, b):
    return lax.dot_general(a, b, (((1,), (0,)), ((), ())), preferred_element_type=F32)


def tiles_of(refs):
    out, base = [], 0
    for ref in refs:
        rows = ref.shape[0]
        for start in range(0, rows, TILE):
            out.append((ref, start, base + start))
        base += rows
    return out


def fold(x, op):
    return op(x.reshape(TILE // 8, 8, x.shape[1]), axis=0)


def store_segments(refs, acc_ref, scale):
    for ref, start, row in tiles_of(refs):
        part = acc_ref[:, row : row + TILE].T
        ref[start : start + TILE, :] = (part if scale is None else part * scale).astype(BF16)


def add_to(acc_ref, row, value, first):
    if first:
        acc_ref[:, row : row + TILE] = value
    else:
        acc_ref[:, row : row + TILE] += value


def probs_kernel(len_ref, q_ref, g_ref, k0, k1, k2, k3, ko, p_hbm, gs_ref, rt_ref, d0, d1, d2, d3, do, s_ref, p_ref, acc_ref, sems):
    base = pl.program_id(0) * RATIO
    tiles = tiles_of((k0, k1, k2, k3, ko))
    tops, totals, copies = {}, {}, []

    def score(r, ref, start, row):
        s = dot_nt(ref[start : start + TILE, :], q_ref[:, r * HEAD : (r + 1) * HEAD])
        if ref is ko:
            key_ids = lax.broadcasted_iota(jnp.int32, s.shape, 0)
            row_ids = lax.broadcasted_iota(jnp.int32, s.shape, 1)
            s = jnp.where(key_ids <= row_ids, s, -jnp.inf)
        s_ref[r % 2, row : row + TILE, :] = s
        part = fold(s, jnp.max)
        tops[r] = jnp.maximum(tops[r], part) if r in tops else part

    def weigh(r, top, row):
        p = jnp.exp2(s_ref[r % 2, row : row + TILE, :] * LOG2 - top)
        p_ref[r, row : row + TILE, :] = p.astype(BF16)
        part = fold(p, jnp.sum)
        totals[r] = totals[r] + part if r in totals else part

    def shrink(r):
        rt = 1.0 / jnp.sum(totals[r], axis=0, keepdims=True)
        rt_ref[r] = jnp.broadcast_to(rt, (8, ROWS))
        rows = lax.broadcasted_iota(jnp.int32, (ROWS, HEAD), 0)
        scaled = g_ref[:, r * HEAD : (r + 1) * HEAD].astype(F32) * jnp.broadcast_to(rt, (HEAD, ROWS)).T
        gs = jnp.where(rows < len_ref[0], scaled, 0.0).astype(BF16)
        gs_ref[:, r * HEAD : (r + 1) * HEAD] = gs
        return gs.T

    for step in range(RATIO + 2):
        now, last, older = step, step - 1, step - 2
        if 0 <= older < RATIO:
            gst = shrink(older)
        if 0 <= last < RATIO:
            top = jnp.max(tops[last], axis=0, keepdims=True) * LOG2
        for ref, start, row in tiles:
            if now < RATIO:
                score(now, ref, start, row)
            if 0 <= last < RATIO:
                weigh(last, top, row)
            if 0 <= older < RATIO:
                add_to(acc_ref, row, dot_nt(gst, p_ref[older, row : row + TILE, :]), older == 0)
        if 0 <= last < RATIO:
            copy = pltpu.make_async_copy(p_ref.at[last], p_hbm.at[base + last], sems.at[last])
            copy.start()
            copies.append(copy)
    store_segments((d0, d1, d2, d3, do), acc_ref, None)
    for copy in copies:
        copy.wait()


def slopes_kernel(q_ref, gs_ref, rt_ref, p_hbm, v0, v1, v2, v3, vo, sl_hbm, d0, d1, d2, d3, do, f_ref, p_ref, sl_ref, acc_ref, in_sems, out_sems):
    base = pl.program_id(0) * RATIO
    tiles = tiles_of((v0, v1, v2, v3, vo))
    deltas, copies, fetches = {}, [], []
    for r in range(RATIO):
        fetch = pltpu.make_async_copy(p_hbm.at[base + r], p_ref.at[r], in_sems.at[r])
        fetch.start()
        fetches.append(fetch)

    def flow(r, ref, start, row):
        f = dot_nt(ref[start : start + TILE, :], gs_ref[:, r * HEAD : (r + 1) * HEAD])
        f_ref[r % 2, row : row + TILE, :] = f
        part = fold(f * p_ref[r, row : row + TILE, :].astype(F32), jnp.sum)
        deltas[r] = deltas[r] + part if r in deltas else part

    for step in range(RATIO + 1):
        now, last = step, step - 1
        if now < RATIO:
            fetches[now].wait()
        if 0 <= last:
            delta = jnp.sum(deltas[last], axis=0, keepdims=True) * rt_ref[last, 0:1, :]
            qt = q_ref[:, last * HEAD : (last + 1) * HEAD].T
        for ref, start, row in tiles:
            if now < RATIO:
                flow(now, ref, start, row)
            if 0 <= last:
                p = p_ref[last, row : row + TILE, :].astype(F32)
                sl = (p * (f_ref[last % 2, row : row + TILE, :] - delta)).astype(BF16)
                sl_ref[last, row : row + TILE, :] = sl
                add_to(acc_ref, row, dot_nt(qt, sl), last == 0)
        if 0 <= last:
            copy = pltpu.make_async_copy(sl_ref.at[last], sl_hbm.at[base + last], out_sems.at[last])
            copy.start()
            copies.append(copy)
    store_segments((d0, d1, d2, d3, do), acc_ref, SCALE)
    for copy in copies:
        copy.wait()


def rows_kernel(len_ref, rt_ref, p_ref, sl_ref, k0, k1, k2, k3, ko, v0, v1, v2, v3, vo, o_ref, dq_ref, kt_ref, vt_ref):
    r = pl.program_id(0) % RATIO

    @pl.when(r == 0)
    def _():
        for ref, start, row in tiles_of((k0, k1, k2, k3, ko)):
            kt_ref[:, row : row + TILE] = ref[start : start + TILE, :].T
        for ref, start, row in tiles_of((v0, v1, v2, v3, vo)):
            vt_ref[:, row : row + TILE] = ref[start : start + TILE, :].T

    out = dot_nn(vt_ref[...], p_ref[0]) * rt_ref[0, 0:1, :]
    row_ids = lax.broadcasted_iota(jnp.int32, out.shape, 1)
    out = jnp.where(row_ids < len_ref[0], out, 0.0)
    o_ref[...] = out.T.astype(BF16)
    dq = dot_nn(kt_ref[...], sl_ref[0]) * SCALE
    dq_ref[...] = dq.T.astype(BF16)


def head_block(h, *_):
    return (0, h)


def group_block(h, *_):
    return (0, h // RATIO)


def plane(h, *_):
    return (h, 0, 0)


def attention_calls(keys):
    count = 2 * RATIO
    head_spec = pl.BlockSpec((ROWS, HEAD), head_block)
    seg_specs = [pl.BlockSpec((SEG, HEAD), group_block)] * 4 + [pl.BlockSpec((ROWS, HEAD), group_block)]
    plane_spec = pl.BlockSpec((1, keys, ROWS), plane)
    rt_spec = pl.BlockSpec((1, 8, ROWS), plane)
    params = pltpu.CompilerParams(dimension_semantics=("arbitrary",), vmem_limit_bytes=VMEM_LIMIT)
    head_shape = jax.ShapeDtypeStruct((ROWS, count * HEAD), BF16)
    seg_shapes = [jax.ShapeDtypeStruct((SEG, 2 * HEAD), BF16)] * 4 + [jax.ShapeDtypeStruct((ROWS, 2 * HEAD), BF16)]
    plane_shape = jax.ShapeDtypeStruct((count, keys, ROWS), BF16)
    rt_shape = jax.ShapeDtypeStruct((count, 8, ROWS), F32)
    work = 4 * count * keys * ROWS * HEAD
    cost = pl.CostEstimate(flops=2 * work, bytes_accessed=20 * 1024 * 1024, transcendentals=count * keys * ROWS)

    five_spec = pl.BlockSpec((ROWS, RATIO * HEAD), lambda l, *_: (0, l))
    wide_specs = [pl.BlockSpec((SEG, HEAD), lambda l, *_: (0, l))] * 4 + [pl.BlockSpec((ROWS, HEAD), lambda l, *_: (0, l))]
    five_rt = pl.BlockSpec((RATIO, 8, ROWS), lambda l, *_: (l, 0, 0))
    hbm = pl.BlockSpec(memory_space=pltpu.HBM)
    five_planes = pltpu.VMEM((RATIO, keys, ROWS), BF16)
    probs = pl.pallas_call(
        probs_kernel,
        grid_spec=pltpu.PrefetchScalarGridSpec(
            num_scalar_prefetch=1,
            grid=(2,),
            in_specs=[five_spec, five_spec] + wide_specs,
            out_specs=[hbm, five_spec, five_rt] + wide_specs,
            scratch_shapes=[
                pltpu.VMEM((2, keys, ROWS), F32),
                five_planes,
                pltpu.VMEM((HEAD, keys), F32),
                pltpu.SemaphoreType.DMA((RATIO,)),
            ],
        ),
        out_shape=[plane_shape, head_shape, rt_shape] + seg_shapes,
        compiler_params=params,
        cost_estimate=cost,
        name="probs",
    )
    slopes = pl.pallas_call(
        slopes_kernel,
        grid=(2,),
        in_specs=[five_spec, five_spec, five_rt, hbm] + wide_specs,
        out_specs=[hbm] + wide_specs,
        scratch_shapes=[
            pltpu.VMEM((2, keys, ROWS), F32),
            five_planes,
            five_planes,
            pltpu.VMEM((HEAD, keys), F32),
            pltpu.SemaphoreType.DMA((RATIO,)),
            pltpu.SemaphoreType.DMA((RATIO,)),
        ],
        out_shape=[plane_shape] + seg_shapes,
        compiler_params=params,
        cost_estimate=cost,
        name="slopes",
    )
    rows = pl.pallas_call(
        rows_kernel,
        grid_spec=pltpu.PrefetchScalarGridSpec(
            num_scalar_prefetch=1,
            grid=(count,),
            in_specs=[rt_spec, plane_spec, plane_spec] + seg_specs + seg_specs,
            out_specs=[head_spec, head_spec],
            scratch_shapes=[pltpu.VMEM((HEAD, keys), BF16)] * 2,
        ),
        out_shape=[head_shape, head_shape],
        compiler_params=params,
        cost_estimate=cost,
        name="rows",
    )
    return probs, slopes, rows


def shift(x, axis, size, by):
    return lax.ppermute(x, axis, [(i, (i + by) % size) for i in range(size)])


def pick(blocks, which):
    low = jnp.where(which == 0, blocks[0], blocks[1])
    high = jnp.where(which == 2, blocks[2], blocks[3])
    return jnp.where(which < 2, low, high)


def group_move(block, source_of, after=None):
    chip = lax.axis_index("x")
    core = lax.axis_index("core")
    wanted = source_of[2 * chip + core]
    mate_wanted = source_of[2 * chip + 1 - core]
    blocks = [block] + [shift(block, "x", 4, by) for by in (1, 2, 3)]
    for_mate = pick(blocks, (chip - mate_wanted // 2) % 4)
    if after is not None:
        for_mate, after = lax.optimization_barrier((for_mate, after))
    from_mate = shift(for_mate, "core", 2, 1)
    mine = pick(blocks, (chip - wanted // 2) % 4)
    return jnp.where(wanted % 2 == core, mine, from_mate), after


def z_exchange(parts):
    return lax.all_to_all(parts, ("z_hi", "z_lo"), 0, 0, tiled=True)


def z_gather(moved):
    parts = moved.reshape(64, 4, 256).transpose(1, 0, 2)
    return z_exchange(jnp.concatenate([parts, parts], axis=0)).reshape(SEG, 256)


def y_gather(segment):
    return [segment] + [shift(segment, "y", 4, by) for by in (1, 2, 3)]


def y_return(segments):
    return [segments[0]] + [shift(segments[by], "y", 4, -by) for by in (1, 2, 3)]


def z_return(segments):
    total = segments[0].astype(F32)
    for segment in segments[1:]:
        total = total + segment.astype(F32)
    parts = z_exchange(total.astype(BF16).reshape(8, 64, 256)).astype(F32)
    block = (parts[:4] + parts[4:]).astype(BF16)
    return block.transpose(1, 0, 2).reshape(64, 1024)


def local(query, own_kv, prompt_kv, d_out, prompt_of, comp_len):
    queries, grads = query[0], d_out[0]
    own_keys, own_values = own_kv[0, :, 0], own_kv[0, :, 1]
    group_ids = lax.iota(jnp.int32, 8)
    owner_of = jnp.sum(jnp.where(prompt_of[None, :] == group_ids[:, None], group_ids[None, :], 0), axis=1)
    probs, slopes, rows = attention_calls(4 * SEG + ROWS)

    key_block, value_block = prompt_kv[0, :, 0], prompt_kv[0, :, 1]
    key_block, value_block = group_move(key_block, prompt_of, value_block)
    key_segment = z_gather(key_block)
    value_block, _ = group_move(value_block, prompt_of)
    key_segment, value_block = lax.optimization_barrier((key_segment, value_block))
    keys = y_gather(key_segment)
    values = y_gather(z_gather(value_block))

    p, scaled, rt, *value_grads = probs(comp_len, queries, grads, *keys, own_keys)
    value_back = y_return(value_grads[:4])
    sl, *key_grads = slopes(queries, scaled, rt, p, *values, own_values)
    key_back = y_return(key_grads[:4])
    value_block, _ = group_move(z_return(value_back), owner_of)
    out, d_query = rows(comp_len, rt, p, sl, *keys, own_keys, *values, own_values)
    key_block, _ = group_move(z_return(key_back), owner_of)

    d_own = jnp.stack([key_grads[4], value_grads[4]], axis=1)
    d_prompt = jnp.stack([key_block, value_block], axis=1)
    return out[None], d_query[None], d_own[None], d_prompt[None]


def solution(mesh):
    fine = Mesh(mesh.devices.reshape(2, 4, 4, 2, 4), ("z_hi", "y", "x", "core", "z_lo"))
    samples, group, rows = ("z_hi", "y", "x", "core"), ("x", "core"), ("z_hi", "y", "z_lo")
    in_specs = (
        P(samples, None, "z_lo"),
        P(samples, None, None, "z_lo"),
        P(group, rows, None, None),
        P(samples, None, "z_lo"),
        P(),
        P(samples),
    )
    out_specs = (
        P(samples, None, "z_lo"),
        P(samples, None, "z_lo"),
        P(samples, None, None, "z_lo"),
        P(group, rows, None, None),
    )
    return jax.shard_map(local, mesh=fine, in_specs=in_specs, out_specs=out_specs, check_vma=False)
```

profile of v0, /device:TPU:1, one launch (start us, length us, event | category | flops | bytes accessed | tf_op | source)
XLA Modules:
  0.0 156.4 jit_solution(2788731815730746211)
XLA Ops:
  0.6 1.5 fusion.5
  2.2 3.7 %collective-permute-start.1 = (bf16[64,1024]{1,0:T(8,128)(2,1)S(1)}, bf16[64,1024]{1,0:T(8,128)(2,1)S(1)}, u32[]{:S(2)}, u32[]{:S(2)}) collective-permute-start(bf16[64,1024]{1,0:T(8,128)(2,1)S(1)} %bitcast.87), channel_id=1, source_target_pairs={{0,16},{8,24},{16,0},{24,8},{1,17},{9,25},{17,1},{25,9},{2,18},{10... | collective-permute-start | bytes 393224 | tf_op jit(solution)/shard_map/ppermute | solution.py:254
  5.8 0.9 collective-permute-start.2
  6.7 0.6 collective-permute-start
  7.3 0.8 select_reduce_fusion
  8.1 1.4 fusion.6
  12.2 1.9 %collective-permute-done = bf16[64,1024]{1,0:T(8,128)(2,1)S(1)} collective-permute-done((bf16[64,1024]{1,0:T(8,128)(2,1)S(1)}, bf16[64,1024]{1,0:T(8,128)(2,1)S(1)}, u32[]{:S(2)}, u32[]{:S(2)}) %collective-permute-start) | collective-permute-done | bytes 131104 | tf_op jit(solution)/shard_map/ppermute | solution.py:254
  14.1 1.1 collective-permute-start.3
  17.8 0.9 collective-permute-start.6
  18.7 0.5 collective-permute-start.5
  19.2 0.6 collective-permute-start.4
  19.9 0.7 pad_maximum_fusion
  20.6 8.2 %all-to-all-start = ((bf16[8,64,256]{2,1,0:T(8,128)(2,1)}), bf16[8,64,256]{2,1,0:T(8,128)(2,1)S(1)}, u32[]{:S(2)}, u32[]{:S(2)}) async-start(bf16[8,64,256]{2,1,0:T(8,128)(2,1)} %pad_maximum_fusion), calls=%async_computation | async-start | bytes 524288 | tf_op jit(solution)/shard_map/all_to_all | solution.py:278
  28.9 1.2 collective-permute-start.7
  30.1 1.0 collective-permute-done.7
  31.1 7.9 %all-to-all-done = bf16[8,64,256]{2,1,0:T(8,128)(2,1)S(1)} async-done(((bf16[8,64,256]{2,1,0:T(8,128)(2,1)}), bf16[8,64,256]{2,1,0:T(8,128)(2,1)S(1)}, u32[]{:S(2)}, u32[]{:S(2)}) %all-to-all-start) | async-done | bytes 262176 | tf_op jit(solution)/shard_map/all_to_all | solution.py:278
  39.0 2.7 %collective-permute-start.10 = (bf16[512,256]{1,0:T(8,128)(2,1)S(1)}, bf16[512,256]{1,0:T(8,128)(2,1)S(1)}, u32[]{:S(2)}, u32[]{:S(2)}) collective-permute-start(bf16[512,256]{1,0:T(8,128)(2,1)S(1)} %bitcast.73), channel_id=1, source_target_pairs={{0,96},{32,0},{64,32},{96,64},{1,97},{33,1},{65,33},{97,65},{2,98}... | collective-permute-start | bytes 786440 | tf_op jit(solution)/shard_map/ppermute | solution.py:254
  42.1 0.7 collective-permute-start.8
  42.8 0.7 pad_maximum_fusion.1
  43.5 3.4 %all-to-all-start.1 = ((bf16[8,64,256]{2,1,0:T(8,128)(2,1)}), bf16[8,64,256]{2,1,0:T(8,128)(2,1)S(1)}, u32[]{:S(2)}, u32[]{:S(2)}) async-start(bf16[8,64,256]{2,1,0:T(8,128)(2,1)} %pad_maximum_fusion.1), calls=%async_computation.1 | async-start | bytes 524288 | tf_op jit(solution)/shard_map/all_to_all | solution.py:278
  46.9 1.5 fusion.4
  49.1 0.7 copy_bitcast_fusion
  49.8 6.5 %all-to-all-done.1 = bf16[8,64,256]{2,1,0:T(8,128)(2,1)S(1)} async-done(((bf16[8,64,256]{2,1,0:T(8,128)(2,1)}), bf16[8,64,256]{2,1,0:T(8,128)(2,1)S(1)}, u32[]{:S(2)}, u32[]{:S(2)}) %all-to-all-start.1) | async-done | bytes 262176 | tf_op jit(solution)/shard_map/all_to_all | solution.py:278
  56.3 2.0 %collective-permute-start.13 = (bf16[512,256]{1,0:T(8,128)(2,1)S(1)}, bf16[512,256]{1,0:T(8,128)(2,1)S(1)}, u32[]{:S(2)}, u32[]{:S(2)}) collective-permute-start(bf16[512,256]{1,0:T(8,128)(2,1)S(1)} %bitcast.78), channel_id=1, source_target_pairs={{0,96},{32,0},{64,32},{96,64},{1,97},{33,1},{65,33},{97,65},{2,98}... | collective-permute-start | bytes 786440 | tf_op jit(solution)/shard_map/ppermute | solution.py:254
  58.3 1.4 collective-permute-start.12
  59.7 0.6 copy-done.2
  60.5 13.6 %probs.1 = (bf16[10,2304,256]{2,1,0:T(8,128)(2,1)}, bf16[256,1280]{1,0:T(8,128)(2,1)}, f32[10,8,256]{2,1,0:T(8,128)}, bf16[512,256]{1,0:T(8,128)(2,1)}, bf16[512...) custom-call(s32[1]{0:T(128)S(6)} %copy.61.len_ref, ...), custom_call_target="tpu_custom_call" | custom-call | flops 6039797760 | bytes 20971520 | tf_op jit(solution)/shard_map/probs/pallas_call | solution.py:318
  74.2 2.7 %collective-permute-start.21 = (bf16[512,256]{1,0:T(8,128)(2,1)}, bf16[512,256]{1,0:T(8,128)(2,1)S(1)}, u32[]{:S(2)}, u32[]{:S(2)}) collective-permute-start(bf16[512,256]{1,0:T(8,128)(2,1)} %get-tuple-element.41), channel_id=1, source_target_pairs={{0,96},{32,0},{64,32},{96,64},{1,97},{33,1},{65,33},{97,65},{2,98}... | collective-permute-start | bytes 786440 | tf_op jit(solution)/shard_map/ppermute | solution.py:254
  78.4 15.8 %slopes.1 = (bf16[10,2304,256]{2,1,0:T(8,128)(2,1)}, bf16[512,256]{1,0:T(8,128)(2,1)}, bf16[512,256]{1,0:T(8,128)(2,1)}, bf16[512,256]{1,0:T(8,128)(2,1)}, bf16[...) custom-call(bf16[256,1280]{1,0:T(8,128)(2,1)} %bitcast.94, bf16[256,1280]{1,0:T(8,128)(2,1)} %get-tuple-element.29.gs_ref, ...), custom_call_target="tpu_custom_call" | custom-call | flops 6039797760 | bytes 20971520 | tf_op jit(solution)/shard_map/slopes/pallas_call | solution.py:320
  94.3 2.6 %collective-permute-start.14 = (bf16[512,256]{1,0:T(8,128)(2,1)}, bf16[512,256]{1,0:T(8,128)(2,1)S(1)}, u32[]{:S(2)}, u32[]{:S(2)}) collective-permute-start(bf16[512,256]{1,0:T(8,128)(2,1)} %get-tuple-element.37), channel_id=1, source_target_pairs={{0,96},{32,0},{64,32},{96,64},{1,97},{33,1},{65,33},{97,65},{2,98}... | collective-permute-start | bytes 786440 | tf_op jit(solution)/shard_map/ppermute | solution.py:254
  96.9 1.4 collective-permute-start.15
  98.3 0.8 add_convert_fusion
  99.2 3.4 %all-to-all-start.3 = ((bf16[8,64,256]{2,1,0:T(8,128)(2,1)}), bf16[8,64,256]{2,1,0:T(8,128)(2,1)S(1)}, u32[]{:S(2)}, u32[]{:S(2)}) async-start(bf16[8,64,256]{2,1,0:T(8,128)(2,1)} %bitcast.22), calls=%async_computation.3 | async-start | bytes 524288 | tf_op jit(solution)/shard_map/all_to_all | solution.py:278
  107.7 1.8 %add_convert_fusion.1 = bf16[512,256]{1,0:T(8,128)(2,1)} fusion(bf16[512,256]{1,0:T(8,128)(2,1)S(1)} %collective-permute-done.16, bf16[512,256]{1,0:T(8,128)(2,1)S(1)} %collective-permute-done.15, bf16[512,256]{1,0:T(8,128)(2,1)S(1)} %collective-permute-done.14, bf16[512,256]{1,0:T(8,128)(2,1)} %get-tuple-element.36), kind=kLoop, calls=%fused_computation.1 | loop fusion | flops 1048576 | bytes 1310720 | tf_op jit(solution)/shard_map/convert_element_type | solution.py:298
  109.5 2.4 %all-to-all-done.3 = bf16[8,64,256]{2,1,0:T(8,128)(2,1)S(1)} async-done(((bf16[8,64,256]{2,1,0:T(8,128)(2,1)}), bf16[8,64,256]{2,1,0:T(8,128)(2,1)S(1)}, u32[]{:S(2)}, u32[]{:S(2)}) %all-to-all-start.3) | async-done | bytes 262176 | tf_op jit(solution)/shard_map/all_to_all | solution.py:278
  111.8 4.2 %all-to-all-start.2 = ((bf16[8,64,256]{2,1,0:T(8,128)(2,1)}), bf16[8,64,256]{2,1,0:T(8,128)(2,1)S(1)}, u32[]{:S(2)}, u32[]{:S(2)}) async-start(bf16[8,64,256]{2,1,0:T(8,128)(2,1)} %bitcast.18), calls=%async_computation.2 | async-start | bytes 524288 | tf_op jit(solution)/shard_map/all_to_all | solution.py:278
  116.1 14.5 %rows.1 = (bf16[256,1280]{1,0:T(8,128)(2,1)}, bf16[256,1280]{1,0:T(8,128)(2,1)}) custom-call(s32[1]{0:T(128)S(6)} %copy.61.len_ref, f32[10,8,256]{2,1,0:T(8,128)} %get-tuple-element.27.rt_ref, bf16[10,2304,256]{2,1,0:T(8,128)(2,1)} %get-tuple-element.28.p_hbm.p_ref, bf16[10,2304,256]{2,1,0:T(8,128)(2,1)} %get-tuple-element.31.sl_ref, ...), custom_call_target="tpu_custom_call" | custom-call | flops 6039797760 | bytes 20971520 | tf_op jit(solution)/shard_map/rows/pallas_call | solution.py:323
  130.6 1.0 copy.37
  131.7 2.2 %collective-permute-start.26 = (bf16[64,1024]{1,0:T(8,128)(2,1)S(1)}, bf16[64,1024]{1,0:T(8,128)(2,1)S(1)}, u32[]{:S(2)}, u32[]{:S(2)}) collective-permute-start(bf16[64,1024]{1,0:T(8,128)(2,1)S(1)} %bitcast.63), channel_id=1, source_target_pairs={{0,24},{8,0},{16,8},{24,16},{1,25},{9,1},{17,9},{25,17},{2,26},{10... | collective-permute-start | bytes 393224 | tf_op jit(solution)/shard_map/ppermute | solution.py:254
  133.9 1.2 collective-permute-start.25
  135.2 2.8 %collective-permute-start.19 = (bf16[64,1024]{1,0:T(8,128)(2,1)S(1)}, bf16[64,1024]{1,0:T(8,128)(2,1)S(1)}, u32[]{:S(2)}, u32[]{:S(2)}) collective-permute-start(bf16[64,1024]{1,0:T(8,128)(2,1)S(1)} %bitcast.68), channel_id=1, source_target_pairs={{0,24},{8,0},{16,8},{24,16},{1,25},{9,1},{17,9},{25,17},{2,26},{10... | collective-permute-start | bytes 393224 | tf_op jit(solution)/shard_map/ppermute | solution.py:254
  137.9 0.5 collective-permute-start.18
  138.6 0.6 collective-permute-done.25
  139.2 1.4 collective-permute-done.24
  140.6 8.8 %collective-permute-start.27 = (bf16[64,1024]{1,0:T(8,128)(2,1)S(1)}, bf16[64,1024]{1,0:T(8,128)(2,1)S(1)}, u32[]{:S(2)}, u32[]{:S(2)}) collective-permute-start(bf16[64,1024]{1,0:T(8,128)(2,1)S(1)} %select_select_fusion), channel_id=1, source_target_pairs={{0,4},{4,0},{1,5},{5,1},{2,6},{6,2},{3,7},{7,3},{8,12},{12,8},{9,1... | collective-permute-start | bytes 393224 | tf_op jit(solution)/shard_map/ppermute | solution.py:254
  149.5 4.9 %collective-permute-start.20 = (bf16[64,1024]{1,0:T(8,128)(2,1)S(1)}, bf16[64,1024]{1,0:T(8,128)(2,1)S(1)}, u32[]{:S(2)}, u32[]{:S(2)}) collective-permute-start(bf16[64,1024]{1,0:T(8,128)(2,1)S(1)} %select_select_fusion.1), channel_id=1, source_target_pairs={{0,4},{4,0},{1,5},{5,1},{2,6},{6,2},{3,7},{7,3},{8,12},{12,8},{9,1... | collective-permute-start | bytes 393224 | tf_op jit(solution)/shard_map/ppermute | solution.py:254
  154.4 0.9 collective-permute-done.20
  155.4 1.0 copy.38
  (72 shorter events, 2.9 us)
Async XLA Ops:
  2.2 10.0 %collective-permute-start.1 = (bf16[64,1024]{1,0:T(8,128)(2,1)S(1)}, bf16[64,1024]{1,0:T(8,128)(2,1)S(1)}, u32[]{:S(2)}, u32[]{:S(2)}) collective-permute-start(bf16[64,1024]{1,0:T(8,128)(2,1)S(1)} %bitcast.87), channel_id=1, source_target_pairs={{0,16},{8,24},{16,0},{24,8},{1,17},{9,25},{17,1},{25,9},{2,18},{10... | collective-permute-start | bytes 393224 | tf_op jit(solution)/shard_map/ppermute | solution.py:254
  5.8 6.3 %collective-permute-start.2 = (bf16[64,1024]{1,0:T(8,128)(2,1)S(1)}, bf16[64,1024]{1,0:T(8,128)(2,1)S(1)}, u32[]{:S(2)}, u32[]{:S(2)}) collective-permute-start(bf16[64,1024]{1,0:T(8,128)(2,1)S(1)} %bitcast.88), channel_id=1, source_target_pairs={{0,24},{8,0},{16,8},{24,16},{1,25},{9,1},{17,9},{25,17},{2,26},{10... | collective-permute-start | bytes 393224 | tf_op jit(solution)/shard_map/ppermute | solution.py:254
  6.7 7.3 %collective-permute-start = (bf16[64,1024]{1,0:T(8,128)(2,1)S(1)}, bf16[64,1024]{1,0:T(8,128)(2,1)S(1)}, u32[]{:S(2)}, u32[]{:S(2)}) collective-permute-start(bf16[64,1024]{1,0:T(8,128)(2,1)S(1)} %bitcast.89), channel_id=1, source_target_pairs={{0,8},{8,16},{16,24},{24,0},{1,9},{9,17},{17,25},{25,1},{2,10},{10... | collective-permute-start | bytes 393224 | tf_op jit(solution)/shard_map/ppermute | solution.py:254
  14.1 5.7 %collective-permute-start.3 = (bf16[64,1024]{1,0:T(8,128)(2,1)S(1)}, bf16[64,1024]{1,0:T(8,128)(2,1)S(1)}, u32[]{:S(2)}, u32[]{:S(2)}) collective-permute-start(bf16[64,1024]{1,0:T(8,128)(2,1)S(1)} %select_select_fusion.4), channel_id=1, source_target_pairs={{0,4},{4,0},{1,5},{5,1},{2,6},{6,2},{3,7},{7,3},{8,12},{12,8},{9,1... | collective-permute-start | bytes 393224 | tf_op jit(solution)/shard_map/ppermute | solution.py:254
  17.8 11.0 %collective-permute-start.6 = (bf16[64,1024]{1,0:T(8,128)(2,1)S(1)}, bf16[64,1024]{1,0:T(8,128)(2,1)S(1)}, u32[]{:S(2)}, u32[]{:S(2)}) collective-permute-start(bf16[64,1024]{1,0:T(8,128)(2,1)S(1)} %bitcast.58), channel_id=1, source_target_pairs={{0,24},{8,0},{16,8},{24,16},{1,25},{9,1},{17,9},{25,17},{2,26},{10... | collective-permute-start | bytes 393224 | tf_op jit(solution)/shard_map/ppermute | solution.py:254
  18.7 10.1 %collective-permute-start.5 = (bf16[64,1024]{1,0:T(8,128)(2,1)S(1)}, bf16[64,1024]{1,0:T(8,128)(2,1)S(1)}, u32[]{:S(2)}, u32[]{:S(2)}) collective-permute-start(bf16[64,1024]{1,0:T(8,128)(2,1)S(1)} %bitcast.59), channel_id=1, source_target_pairs={{0,16},{8,24},{16,0},{24,8},{1,17},{9,25},{17,1},{25,9},{2,18},{10... | collective-permute-start | bytes 393224 | tf_op jit(solution)/shard_map/ppermute | solution.py:254
  19.2 9.6 %collective-permute-start.4 = (bf16[64,1024]{1,0:T(8,128)(2,1)S(1)}, bf16[64,1024]{1,0:T(8,128)(2,1)S(1)}, u32[]{:S(2)}, u32[]{:S(2)}) collective-permute-start(bf16[64,1024]{1,0:T(8,128)(2,1)S(1)} %bitcast.60), channel_id=1, source_target_pairs={{0,8},{8,16},{16,24},{24,0},{1,9},{9,17},{17,25},{25,1},{2,10},{10... | collective-permute-start | bytes 393224 | tf_op jit(solution)/shard_map/ppermute | solution.py:254
  20.6 18.4 %all-to-all-start = ((bf16[8,64,256]{2,1,0:T(8,128)(2,1)}), bf16[8,64,256]{2,1,0:T(8,128)(2,1)S(1)}, u32[]{:S(2)}, u32[]{:S(2)}) async-start(bf16[8,64,256]{2,1,0:T(8,128)(2,1)} %pad_maximum_fusion), calls=%async_computation | async-start | bytes 524288 | tf_op jit(solution)/shard_map/all_to_all | solution.py:278
  28.9 2.2 %collective-permute-start.7 = (bf16[64,1024]{1,0:T(8,128)(2,1)S(1)}, bf16[64,1024]{1,0:T(8,128)(2,1)S(1)}, u32[]{:S(2)}, u32[]{:S(2)}) collective-permute-start(bf16[64,1024]{1,0:T(8,128)(2,1)S(1)} %select_select_fusion.2), channel_id=1, source_target_pairs={{0,4},{4,0},{1,5},{5,1},{2,6},{6,2},{3,7},{7,3},{8,12},{12,8},{9,1... | collective-permute-start | bytes 393224 | tf_op jit(solution)/shard_map/ppermute | solution.py:254
  39.0 20.7 %copy-start = (bf16[8,64,256]{2,1,0:T(8,128)(2,1)}, bf16[8,64,256]{2,1,0:T(8,128)(2,1)S(1)}, u32[]{:S(2)}) copy-start(bf16[8,64,256]{2,1,0:T(8,128)(2,1)S(1)} %all-to-all-done) | copy-start | bytes 786436
  39.0 20.7 %collective-permute-start.10 = (bf16[512,256]{1,0:T(8,128)(2,1)S(1)}, bf16[512,256]{1,0:T(8,128)(2,1)S(1)}, u32[]{:S(2)}, u32[]{:S(2)}) collective-permute-start(bf16[512,256]{1,0:T(8,128)(2,1)S(1)} %bitcast.73), channel_id=1, source_target_pairs={{0,96},{32,0},{64,32},{96,64},{1,97},{33,1},{65,33},{97,65},{2,98}... | collective-permute-start | bytes 786440 | tf_op jit(solution)/shard_map/ppermute | solution.py:254
  41.7 18.0 %collective-permute-start.9 = (bf16[512,256]{1,0:T(8,128)(2,1)S(1)}, bf16[512,256]{1,0:T(8,128)(2,1)S(1)}, u32[]{:S(2)}, u32[]{:S(2)}) collective-permute-start(bf16[512,256]{1,0:T(8,128)(2,1)S(1)} %bitcast.74), channel_id=1, source_target_pairs={{0,64},{32,96},{64,0},{96,32},{1,65},{33,97},{65,1},{97,33},{2,66}... | collective-permute-start | bytes 786440 | tf_op jit(solution)/shard_map/ppermute | solution.py:254
  42.1 17.6 %collective-permute-start.8 = (bf16[512,256]{1,0:T(8,128)(2,1)S(1)}, bf16[512,256]{1,0:T(8,128)(2,1)S(1)}, u32[]{:S(2)}, u32[]{:S(2)}) collective-permute-start(bf16[512,256]{1,0:T(8,128)(2,1)S(1)} %bitcast.75), channel_id=1, source_target_pairs={{0,32},{32,64},{64,96},{96,0},{1,33},{33,65},{65,97},{97,1},{2,34}... | collective-permute-start | bytes 786440 | tf_op jit(solution)/shard_map/ppermute | solution.py:254
  43.5 12.8 %all-to-all-start.1 = ((bf16[8,64,256]{2,1,0:T(8,128)(2,1)}), bf16[8,64,256]{2,1,0:T(8,128)(2,1)S(1)}, u32[]{:S(2)}, u32[]{:S(2)}) async-start(bf16[8,64,256]{2,1,0:T(8,128)(2,1)} %pad_maximum_fusion.1), calls=%async_computation.1 | async-start | bytes 524288 | tf_op jit(solution)/shard_map/all_to_all | solution.py:278
  56.3 21.3 %copy-start.1 = (bf16[8,64,256]{2,1,0:T(8,128)(2,1)}, bf16[8,64,256]{2,1,0:T(8,128)(2,1)S(1)}, u32[]{:S(2)}) copy-start(bf16[8,64,256]{2,1,0:T(8,128)(2,1)S(1)} %all-to-all-done.1) | copy-start | bytes 786436
  56.3 21.0 %collective-permute-start.13 = (bf16[512,256]{1,0:T(8,128)(2,1)S(1)}, bf16[512,256]{1,0:T(8,128)(2,1)S(1)}, u32[]{:S(2)}, u32[]{:S(2)}) collective-permute-start(bf16[512,256]{1,0:T(8,128)(2,1)S(1)} %bitcast.78), channel_id=1, source_target_pairs={{0,96},{32,0},{64,32},{96,64},{1,97},{33,1},{65,33},{97,65},{2,98}... | collective-permute-start | bytes 786440 | tf_op jit(solution)/shard_map/ppermute | solution.py:254
  58.3 19.3 %collective-permute-start.12 = (bf16[512,256]{1,0:T(8,128)(2,1)S(1)}, bf16[512,256]{1,0:T(8,128)(2,1)S(1)}, u32[]{:S(2)}, u32[]{:S(2)}) collective-permute-start(bf16[512,256]{1,0:T(8,128)(2,1)S(1)} %bitcast.79), channel_id=1, source_target_pairs={{0,64},{32,96},{64,0},{96,32},{1,65},{33,97},{65,1},{97,33},{2,66}... | collective-permute-start | bytes 786440 | tf_op jit(solution)/shard_map/ppermute | solution.py:254
  59.7 0.7 copy-start.2
  59.7 17.9 %collective-permute-start.11 = (bf16[512,256]{1,0:T(8,128)(2,1)S(1)}, bf16[512,256]{1,0:T(8,128)(2,1)S(1)}, u32[]{:S(2)}, u32[]{:S(2)}) collective-permute-start(bf16[512,256]{1,0:T(8,128)(2,1)S(1)} %bitcast.80), channel_id=1, source_target_pairs={{0,32},{32,64},{64,96},{96,0},{1,33},{33,65},{65,97},{97,1},{2,34}... | collective-permute-start | bytes 786440 | tf_op jit(solution)/shard_map/ppermute | solution.py:254
  59.7 0.8 copy-start.3
  59.7 0.8 copy-start.4
  74.2 24.1 %copy-start.8 = (bf16[512,256]{1,0:T(8,128)(2,1)S(1)}, bf16[512,256]{1,0:T(8,128)(2,1)}, u32[]{:S(2)}) copy-start(bf16[512,256]{1,0:T(8,128)(2,1)} %get-tuple-element.40) | copy-start | bytes 786436
  74.2 24.1 %collective-permute-start.21 = (bf16[512,256]{1,0:T(8,128)(2,1)}, bf16[512,256]{1,0:T(8,128)(2,1)S(1)}, u32[]{:S(2)}, u32[]{:S(2)}) collective-permute-start(bf16[512,256]{1,0:T(8,128)(2,1)} %get-tuple-element.41), channel_id=1, source_target_pairs={{0,96},{32,0},{64,32},{96,64},{1,97},{33,1},{65,33},{97,65},{2,98}... | collective-permute-start | bytes 786440 | tf_op jit(solution)/shard_map/ppermute | solution.py:254
  76.9 21.4 %collective-permute-start.22 = (bf16[512,256]{1,0:T(8,128)(2,1)}, bf16[512,256]{1,0:T(8,128)(2,1)S(1)}, u32[]{:S(2)}, u32[]{:S(2)}) collective-permute-start(bf16[512,256]{1,0:T(8,128)(2,1)} %get-tuple-element.42), channel_id=1, source_target_pairs={{0,64},{32,96},{64,0},{96,32},{1,65},{33,97},{65,1},{97,33},{2,66}... | collective-permute-start | bytes 786440 | tf_op jit(solution)/shard_map/ppermute | solution.py:254
  77.2 0.7 copy-start.5
  77.2 21.1 %collective-permute-start.23 = (bf16[512,256]{1,0:T(8,128)(2,1)}, bf16[512,256]{1,0:T(8,128)(2,1)S(1)}, u32[]{:S(2)}, u32[]{:S(2)}) collective-permute-start(bf16[512,256]{1,0:T(8,128)(2,1)} %get-tuple-element.43), channel_id=1, source_target_pairs={{0,32},{32,64},{64,96},{96,0},{1,33},{33,65},{65,97},{97,1},{2,34}... | collective-permute-start | bytes 786440 | tf_op jit(solution)/shard_map/ppermute | solution.py:254
  77.6 0.7 copy-start.6
  77.6 0.8 copy-start.7
  94.3 13.4 %collective-permute-start.14 = (bf16[512,256]{1,0:T(8,128)(2,1)}, bf16[512,256]{1,0:T(8,128)(2,1)S(1)}, u32[]{:S(2)}, u32[]{:S(2)}) collective-permute-start(bf16[512,256]{1,0:T(8,128)(2,1)} %get-tuple-element.37), channel_id=1, source_target_pairs={{0,96},{32,0},{64,32},{96,64},{1,97},{33,1},{65,33},{97,65},{2,98}... | collective-permute-start | bytes 786440 | tf_op jit(solution)/shard_map/ppermute | solution.py:254
  96.9 10.8 %collective-permute-start.15 = (bf16[512,256]{1,0:T(8,128)(2,1)}, bf16[512,256]{1,0:T(8,128)(2,1)S(1)}, u32[]{:S(2)}, u32[]{:S(2)}) collective-permute-start(bf16[512,256]{1,0:T(8,128)(2,1)} %get-tuple-element.38), channel_id=1, source_target_pairs={{0,64},{32,96},{64,0},{96,32},{1,65},{33,97},{65,1},{97,33},{2,66}... | collective-permute-start | bytes 786440 | tf_op jit(solution)/shard_map/ppermute | solution.py:254
  98.3 9.4 %collective-permute-start.16 = (bf16[512,256]{1,0:T(8,128)(2,1)}, bf16[512,256]{1,0:T(8,128)(2,1)S(1)}, u32[]{:S(2)}, u32[]{:S(2)}) collective-permute-start(bf16[512,256]{1,0:T(8,128)(2,1)} %get-tuple-element.39), channel_id=1, source_target_pairs={{0,32},{32,64},{64,96},{96,0},{1,33},{33,65},{65,97},{97,1},{2,34}... | collective-permute-start | bytes 786440 | tf_op jit(solution)/shard_map/ppermute | solution.py:254
  99.2 12.7 %all-to-all-start.3 = ((bf16[8,64,256]{2,1,0:T(8,128)(2,1)}), bf16[8,64,256]{2,1,0:T(8,128)(2,1)S(1)}, u32[]{:S(2)}, u32[]{:S(2)}) async-start(bf16[8,64,256]{2,1,0:T(8,128)(2,1)} %bitcast.22), calls=%async_computation.3 | async-start | bytes 524288 | tf_op jit(solution)/shard_map/all_to_all | solution.py:278
  111.8 23.3 %all-to-all-start.2 = ((bf16[8,64,256]{2,1,0:T(8,128)(2,1)}), bf16[8,64,256]{2,1,0:T(8,128)(2,1)S(1)}, u32[]{:S(2)}, u32[]{:S(2)}) async-start(bf16[8,64,256]{2,1,0:T(8,128)(2,1)} %bitcast.18), calls=%async_computation.2 | async-start | bytes 524288 | tf_op jit(solution)/shard_map/all_to_all | solution.py:278
  116.1 14.5 %copy-start.9 = (bf16[256,256]{1,0:T(8,128)(2,1)S(1)}, bf16[256,256]{1,0:T(8,128)(2,1)}, u32[]{:S(2)}) copy-start(bf16[256,256]{1,0:T(8,128)(2,1)} %get-tuple-element.35) | copy-start | bytes 393220
  116.1 14.5 %copy-start.10 = (bf16[256,256]{1,0:T(8,128)(2,1)S(1)}, bf16[256,256]{1,0:T(8,128)(2,1)}, u32[]{:S(2)}) copy-start(bf16[256,256]{1,0:T(8,128)(2,1)} %get-tuple-element.34) | copy-start | bytes 393220
  131.7 6.8 %collective-permute-start.26 = (bf16[64,1024]{1,0:T(8,128)(2,1)S(1)}, bf16[64,1024]{1,0:T(8,128)(2,1)S(1)}, u32[]{:S(2)}, u32[]{:S(2)}) collective-permute-start(bf16[64,1024]{1,0:T(8,128)(2,1)S(1)} %bitcast.63), channel_id=1, source_target_pairs={{0,24},{8,0},{16,8},{24,16},{1,25},{9,1},{17,9},{25,17},{2,26},{10... | collective-permute-start | bytes 393224 | tf_op jit(solution)/shard_map/ppermute | solution.py:254
  133.9 5.4 %collective-permute-start.25 = (bf16[64,1024]{1,0:T(8,128)(2,1)S(1)}, bf16[64,1024]{1,0:T(8,128)(2,1)S(1)}, u32[]{:S(2)}, u32[]{:S(2)}) collective-permute-start(bf16[64,1024]{1,0:T(8,128)(2,1)S(1)} %bitcast.64), channel_id=1, source_target_pairs={{0,16},{8,24},{16,0},{24,8},{1,17},{9,25},{17,1},{25,9},{2,18},{10... | collective-permute-start | bytes 393224 | tf_op jit(solution)/shard_map/ppermute | solution.py:254
  135.1 5.5 %collective-permute-start.24 = (bf16[64,1024]{1,0:T(8,128)(2,1)S(1)}, bf16[64,1024]{1,0:T(8,128)(2,1)S(1)}, u32[]{:S(2)}, u32[]{:S(2)}) collective-permute-start(bf16[64,1024]{1,0:T(8,128)(2,1)S(1)} %bitcast.65), channel_id=1, source_target_pairs={{0,8},{8,16},{16,24},{24,0},{1,9},{9,17},{17,25},{25,1},{2,10},{10... | collective-permute-start | bytes 393224 | tf_op jit(solution)/shard_map/ppermute | solution.py:254
  135.2 14.3 %collective-permute-start.19 = (bf16[64,1024]{1,0:T(8,128)(2,1)S(1)}, bf16[64,1024]{1,0:T(8,128)(2,1)S(1)}, u32[]{:S(2)}, u32[]{:S(2)}) collective-permute-start(bf16[64,1024]{1,0:T(8,128)(2,1)S(1)} %bitcast.68), channel_id=1, source_target_pairs={{0,24},{8,0},{16,8},{24,16},{1,25},{9,1},{17,9},{25,17},{2,26},{10... | collective-permute-start | bytes 393224 | tf_op jit(solution)/shard_map/ppermute | solution.py:254
  137.9 11.5 %collective-permute-start.18 = (bf16[64,1024]{1,0:T(8,128)(2,1)S(1)}, bf16[64,1024]{1,0:T(8,128)(2,1)S(1)}, u32[]{:S(2)}, u32[]{:S(2)}) collective-permute-start(bf16[64,1024]{1,0:T(8,128)(2,1)S(1)} %bitcast.69), channel_id=1, source_target_pairs={{0,16},{8,24},{16,0},{24,8},{1,17},{9,25},{17,1},{25,9},{2,18},{10... | collective-permute-start | bytes 393224 | tf_op jit(solution)/shard_map/ppermute | solution.py:254
  138.5 11.0 %collective-permute-start.17 = (bf16[64,1024]{1,0:T(8,128)(2,1)S(1)}, bf16[64,1024]{1,0:T(8,128)(2,1)S(1)}, u32[]{:S(2)}, u32[]{:S(2)}) collective-permute-start(bf16[64,1024]{1,0:T(8,128)(2,1)S(1)} %bitcast.70), channel_id=1, source_target_pairs={{0,8},{8,16},{16,24},{24,0},{1,9},{9,17},{17,25},{25,1},{2,10},{10... | collective-permute-start | bytes 393224 | tf_op jit(solution)/shard_map/ppermute | solution.py:254
  140.6 13.7 %collective-permute-start.27 = (bf16[64,1024]{1,0:T(8,128)(2,1)S(1)}, bf16[64,1024]{1,0:T(8,128)(2,1)S(1)}, u32[]{:S(2)}, u32[]{:S(2)}) collective-permute-start(bf16[64,1024]{1,0:T(8,128)(2,1)S(1)} %select_select_fusion), channel_id=1, source_target_pairs={{0,4},{4,0},{1,5},{5,1},{2,6},{6,2},{3,7},{7,3},{8,12},{12,8},{9,1... | collective-permute-start | bytes 393224 | tf_op jit(solution)/shard_map/ppermute | solution.py:254
  149.5 5.8 %collective-permute-start.20 = (bf16[64,1024]{1,0:T(8,128)(2,1)S(1)}, bf16[64,1024]{1,0:T(8,128)(2,1)S(1)}, u32[]{:S(2)}, u32[]{:S(2)}) collective-permute-start(bf16[64,1024]{1,0:T(8,128)(2,1)S(1)} %select_select_fusion.1), channel_id=1, source_target_pairs={{0,4},{4,0},{1,5},{5,1},{2,6},{6,2},{3,7},{7,3},{8,12},{12,8},{9,1... | collective-permute-start | bytes 393224 | tf_op jit(solution)/shard_map/ppermute | solution.py:254
where the time goes:
time: 157 us; the launch traced here: 156 us
  starting transfers between devices  63.7 us (41%)
  Pallas kernels  44 us (28%)
  waiting for transfers between devices  22.5 us (14%)
  between operations  12 us (8%)
  local copies, waits for them, and re-layouts  8.84 us (6%)
  other arithmetic  5.38 us (3%)
    ppermute x28, starting transfers between devices, shift(): return lax.ppermute(x, axis, [(i, (i + by) % size) for i in range(size)])  44.5 us
    all_to_all x4, starting transfers between devices, z_exchange(): return lax.all_to_all(parts, ('z_hi', 'z_lo'), 0, 0, tiled=True)  19.2 us
    all_to_all x4, waiting for transfers between devices, z_exchange(): return lax.all_to_all(parts, ('z_hi', 'z_lo'), 0, 0, tiled=True)  16.7 us
    pallas_call x1, Pallas kernels, local(): sl, *key_grads = slopes(queries, scaled, rt, p, *values, own_values)  15.8 us
    pallas_call x1, Pallas kernels, local(): rows(comp_len, rt, p, sl, *keys, own_keys, *values, own_values)  14.5 us
    pallas_call x1, Pallas kernels, local(): probs(comp_len, queries, grads, *keys, own_keys)  13.6 us
    ppermute x28, waiting for transfers between devices, shift(): return lax.ppermute(x, axis, [(i, (i + by) % size) for i in range(size)])  5.81 us
    unnamed x26, local copies, waits for them, and re-layouts  3.69 us
  transfers between devices with their start and end apart: 32, of which 8 were waited for; matrix products, arithmetic and copies ran while one was open for 6% of the time, Pallas kernels for 28%

commit v1 on v0

v1 whole, which is shorter than its diff:
```python
import math
import jax
import jax.numpy as jnp
from jax import lax
from jax.experimental import pallas as pl
from jax.experimental.pallas import tpu as pltpu
from jax.sharding import Mesh, PartitionSpec as P

HEADS = 40
KV_HEADS = 8
HEAD = 128
RATIO = HEADS // KV_HEADS
ROWS = 256
SEG = 512
TILE = 256
SCALE = HEAD ** (-0.5)
LOG2 = SCALE * math.log2(math.e)
VMEM_LIMIT = 60 * 1024 * 1024

F32 = jnp.float32
BF16 = jnp.bfloat16


def dot_nt(a, b):
    return lax.dot_general(a, b, (((1,), (1,)), ((), ())), preferred_element_type=F32)


def dot_nn(a, b):
    return lax.dot_general(a, b, (((1,), (0,)), ((), ())), preferred_element_type=F32)


def tiles_of(refs):
    out, base = [], 0
    for ref in refs:
        rows = ref.shape[0]
        for start in range(0, rows, TILE):
            out.append((ref, start, base + start))
        base += rows
    return out


def fold(x, op):
    return op(x.reshape(TILE // 8, 8, x.shape[1]), axis=0)


def store_segments(refs, acc_ref, scale):
    for ref, start, row in tiles_of(refs):
        part = acc_ref[:, row : row + TILE].T
        ref[start : start + TILE, :] = (part if scale is None else part * scale).astype(BF16)


def add_to(acc_ref, row, value, first):
    if first:
        acc_ref[:, row : row + TILE] = value
    else:
        acc_ref[:, row : row + TILE] += value


def probs_kernel(len_ref, q_ref, g_ref, k0, k1, k2, k3, ko, p_hbm, gs_ref, rt_ref, d0, d1, d2, d3, do, s_ref, p_ref, acc_ref, sems):
    base = pl.program_id(0) * RATIO
    tiles = tiles_of((k0, k1, k2, k3, ko))
    tops, totals, copies = {}, {}, []

    def score(r, ref, start, row):
        s = dot_nt(ref[start : start + TILE, :], q_ref[:, r * HEAD : (r + 1) * HEAD])
        if ref is ko:
            key_ids = lax.broadcasted_iota(jnp.int32, s.shape, 0)
            row_ids = lax.broadcasted_iota(jnp.int32, s.shape, 1)
            s = jnp.where(key_ids <= row_ids, s, -jnp.inf)
        s_ref[r % 2, row : row + TILE, :] = s
        part = fold(s, jnp.max)
        tops[r] = jnp.maximum(tops[r], part) if r in tops else part

    def weigh(r, top, row):
        p = jnp.exp2(s_ref[r % 2, row : row + TILE, :] * LOG2 - top)
        p_ref[r, row : row + TILE, :] = p.astype(BF16)
        part = fold(p, jnp.sum)
        totals[r] = totals[r] + part if r in totals else part

    def shrink(r):
        rt = 1.0 / jnp.sum(totals[r], axis=0, keepdims=True)
        rt_ref[r] = jnp.broadcast_to(rt, (8, ROWS))
        rows = lax.broadcasted_iota(jnp.int32, (ROWS, HEAD), 0)
        scaled = g_ref[:, r * HEAD : (r + 1) * HEAD].astype(F32) * jnp.broadcast_to(rt, (HEAD, ROWS)).T
        gs = jnp.where(rows < len_ref[0], scaled, 0.0).astype(BF16)
        gs_ref[:, r * HEAD : (r + 1) * HEAD] = gs
        return gs.T

    for step in range(RATIO + 2):
        now, last, older = step, step - 1, step - 2
        if 0 <= older < RATIO:
            gst = shrink(older)
        if 0 <= last < RATIO:
            top = jnp.max(tops[last], axis=0, keepdims=True) * LOG2
        for ref, start, row in tiles:
            if now < RATIO:
                score(now, ref, start, row)
            if 0 <= last < RATIO:
                weigh(last, top, row)
            if 0 <= older < RATIO:
                add_to(acc_ref, row, dot_nt(gst, p_ref[older, row : row + TILE, :]), older == 0)
        if 0 <= last < RATIO:
            copy = pltpu.make_async_copy(p_ref.at[last], p_hbm.at[base + last], sems.at[last])
            copy.start()
            copies.append(copy)
    store_segments((d0, d1, d2, d3, do), acc_ref, None)
    for copy in copies:
        copy.wait()


def slopes_kernel(q_ref, gs_ref, rt_ref, p_hbm, k0, k1, k2, k3, ko, v0, v1, v2, v3, vo, dq_ref, d0, d1, d2, d3, do, f_ref, p_ref, sl_ref, acc_ref, kt_ref, sems):
    base = pl.program_id(0) * RATIO
    tiles = tiles_of((v0, v1, v2, v3, vo))
    deltas, fetches = {}, []
    for r in range(RATIO):
        fetch = pltpu.make_async_copy(p_hbm.at[base + r], p_ref.at[r], sems.at[r])
        fetch.start()
        fetches.append(fetch)
    for ref, start, row in tiles_of((k0, k1, k2, k3, ko)):
        kt_ref[:, row : row + TILE] = ref[start : start + TILE, :].T

    def flow(r, ref, start, row):
        f = dot_nt(ref[start : start + TILE, :], gs_ref[:, r * HEAD : (r + 1) * HEAD])
        f_ref[r % 2, row : row + TILE, :] = f
        part = fold(f * p_ref[r, row : row + TILE, :].astype(F32), jnp.sum)
        deltas[r] = deltas[r] + part if r in deltas else part

    for step in range(RATIO + 2):
        now, last, older = step, step - 1, step - 2
        if now < RATIO:
            fetches[now].wait()
        if 0 <= last < RATIO:
            delta = jnp.sum(deltas[last], axis=0, keepdims=True) * rt_ref[last, 0:1, :]
            qt = q_ref[:, last * HEAD : (last + 1) * HEAD].T
        if 0 <= older < RATIO:
            dq = dot_nn(kt_ref[...], sl_ref[older % 2]) * SCALE
            dq_ref[:, older * HEAD : (older + 1) * HEAD] = dq.T.astype(BF16)
        for ref, start, row in tiles:
            if now < RATIO:
                flow(now, ref, start, row)
            if 0 <= last < RATIO:
                p = p_ref[last, row : row + TILE, :].astype(F32)
                sl = (p * (f_ref[last % 2, row : row + TILE, :] - delta)).astype(BF16)
                sl_ref[last % 2, row : row + TILE, :] = sl
                add_to(acc_ref, row, dot_nt(qt, sl), last == 0)
    store_segments((d0, d1, d2, d3, do), acc_ref, SCALE)


def rows_kernel(base, len_ref, rt_ref, p_hbm, v0, v1, v2, v3, vo, *rest):
    o_ref, p_ref, vt_ref, sems = rest[-4:]
    fetches = []
    for r in range(RATIO):
        fetch = pltpu.make_async_copy(p_hbm.at[base + r], p_ref.at[r], sems.at[r])
        fetch.start()
        fetches.append(fetch)
    for ref, start, row in tiles_of((v0, v1, v2, v3, vo)):
        vt_ref[:, row : row + TILE] = ref[start : start + TILE, :].T
    for r in range(RATIO):
        fetches[r].wait()
        out = dot_nn(vt_ref[...], p_ref[r]) * rt_ref[r, 0:1, :]
        row_ids = lax.broadcasted_iota(jnp.int32, out.shape, 1)
        out = jnp.where(row_ids < len_ref[0], out, 0.0)
        o_ref[:, r * HEAD : (r + 1) * HEAD] = out.T.astype(BF16)


def attention_calls(keys):
    count = 2 * RATIO
    columns = lambda l, *_: (0, l)
    five_spec = pl.BlockSpec((ROWS, RATIO * HEAD), columns)
    own_spec = pl.BlockSpec((ROWS, HEAD), columns)
    seg_specs = [pl.BlockSpec((SEG, HEAD), columns)] * 4 + [own_spec]
    five_rt = pl.BlockSpec((RATIO, 8, ROWS), lambda l, *_: (l, 0, 0))
    hbm = pl.BlockSpec(memory_space=pltpu.HBM)
    five_planes = pltpu.VMEM((RATIO, keys, ROWS), BF16)
    score_planes = pltpu.VMEM((2, keys, ROWS), F32)
    sums = pltpu.VMEM((HEAD, keys), F32)
    sems = pltpu.SemaphoreType.DMA((RATIO,))
    params = pltpu.CompilerParams(dimension_semantics=("arbitrary",), vmem_limit_bytes=VMEM_LIMIT)
    head_shape = jax.ShapeDtypeStruct((ROWS, count * HEAD), BF16)
    own_shape = jax.ShapeDtypeStruct((ROWS, 2 * HEAD), BF16)
    seg_shapes = [jax.ShapeDtypeStruct((SEG, 2 * HEAD), BF16)] * 4 + [own_shape]
    plane_shape = jax.ShapeDtypeStruct((count, keys, ROWS), BF16)
    rt_shape = jax.ShapeDtypeStruct((count, 8, ROWS), F32)
    work = 4 * count * keys * ROWS * HEAD

    def cost(flops, exps):
        return pl.CostEstimate(flops=flops, bytes_accessed=20 * 1024 * 1024, transcendentals=exps)

    probs = pl.pallas_call(
        probs_kernel,
        grid_spec=pltpu.PrefetchScalarGridSpec(
            num_scalar_prefetch=1,
            grid=(2,),
            in_specs=[five_spec, five_spec] + seg_specs,
            out_specs=[hbm, five_spec, five_rt] + seg_specs,
            scratch_shapes=[score_planes, five_planes, sums, sems],
        ),
        out_shape=[plane_shape, head_shape, rt_shape] + seg_shapes,
        compiler_params=params,
        cost_estimate=cost(2 * work, count * keys * ROWS),
        name="probs",
    )
    slopes = pl.pallas_call(
        slopes_kernel,
        grid=(2,),
        in_specs=[five_spec, five_spec, five_rt, hbm] + seg_specs + seg_specs,
        out_specs=[five_spec] + seg_specs,
        scratch_shapes=[
            score_planes,
            five_planes,
            pltpu.VMEM((2, keys, ROWS), BF16),
            sums,
            pltpu.VMEM((HEAD, keys), BF16),
            sems,
        ],
        out_shape=[head_shape] + seg_shapes,
        compiler_params=params,
        cost_estimate=cost(2 * work, 0),
        name="slopes",
    )

    def rows(half, before, *operands):
        pinned = lambda spec: pl.BlockSpec(spec.block_shape, lambda i, *_: spec.index_map(half))
        return pl.pallas_call(
            lambda *refs: rows_kernel(half * RATIO, *refs),
            grid_spec=pltpu.PrefetchScalarGridSpec(
                num_scalar_prefetch=1,
                grid=(1,),
                in_specs=[pinned(five_rt), hbm]
                + [pinned(x) for x in seg_specs]
                + [pl.BlockSpec(memory_space=pl.ANY)] * len(before),
                out_specs=pinned(five_spec),
                scratch_shapes=[five_planes, pltpu.VMEM((HEAD, keys), BF16), sems],
            ),
            out_shape=head_shape,
            input_output_aliases={len(operands): 0} if before else {},
            compiler_params=params,
            cost_estimate=cost(work // 2, 0) if before else pl.CostEstimate(flops=1, bytes_accessed=1, transcendentals=0),
            name="rows",
        )(*operands, *before)

    return probs, slopes, rows


def shift(x, axis, size, by):
    return lax.ppermute(x, axis, [(i, (i + by) % size) for i in range(size)])


def route(chip, core, source_of):
    spot = 2 * chip + core
    wanted, mate_wanted = source_of[spot], source_of[spot ^ 1]

    def by_distance(source):
        distance = (chip + 4 - lax.shift_right_logical(source, 1)) & 3
        return distance == 0, distance == 2, distance < 2

    return by_distance(mate_wanted), by_distance(wanted), (wanted & 1) == core


def pick(blocks, selectors):
    first, third, low = selectors
    return jnp.where(low, jnp.where(first, blocks[0], blocks[1]), jnp.where(third, blocks[2], blocks[3]))


def x_spread(block):
    return [block] + [shift(block, "x", 4, by) for by in (1, 2, 3)]


def core_pick(blocks, routes, after=None):
    mate_route, own_route, same_core = routes
    for_mate = pick(blocks, mate_route)
    if after is not None:
        for_mate, after = lax.optimization_barrier((for_mate, after))
    from_mate = shift(for_mate, "core", 2, 1)
    return jnp.where(same_core, pick(blocks, own_route), from_mate), after


def z_exchange(parts):
    return lax.all_to_all(parts, ("z_hi", "z_lo"), 0, 0, tiled=True)


def z_gather(moved):
    parts = moved.reshape(64, 4, 256).transpose(1, 0, 2)
    return z_exchange(jnp.concatenate([parts, parts], axis=0)).reshape(SEG, 256)


def y_gather(segment):
    return [segment] + [shift(segment, "y", 4, by) for by in (1, 2, 3)]


def y_return(segments):
    return [segments[0]] + [shift(segments[by], "y", 4, -by) for by in (1, 2, 3)]


def sum_segments(segments):
    total = segments[0].astype(F32)
    for segment in segments[1:]:
        total = total + segment.astype(F32)
    return total.astype(BF16).reshape(8, 64, 256)


def z_sum(parts):
    parts = parts.astype(F32)
    block = (parts[:4] + parts[4:]).astype(BF16)
    return block.transpose(1, 0, 2).reshape(64, 1024)


def local(query, own_kv, prompt_kv, d_out, prompt_of, comp_len):
    queries, grads = query[0], d_out[0]
    own_keys, own_values = own_kv[0, :, 0], own_kv[0, :, 1]
    group_ids = lax.iota(jnp.int32, 8)
    owner_of = jnp.sum(jnp.where(prompt_of[None, :] == group_ids[:, None], group_ids[None, :], 0), axis=1)
    probs, slopes, rows = attention_calls(4 * SEG + ROWS)

    chip, core = lax.axis_index("x"), lax.axis_index("core")
    prompt_route, owner_route = route(chip, core, prompt_of), route(chip, core, owner_of)

    key_block, value_block = prompt_kv[0, :, 0], prompt_kv[0, :, 1]
    key_block, value_block = core_pick(x_spread(key_block), prompt_route, value_block)
    key_segment = z_gather(key_block)
    value_block, _ = core_pick(x_spread(value_block), prompt_route)
    key_segment, value_block = lax.optimization_barrier((key_segment, value_block))
    keys = y_gather(key_segment)
    value_segment = z_gather(value_block)
    values = y_gather(value_segment)
    queries, value_segment, owner_route = lax.optimization_barrier((queries, value_segment, owner_route))

    p, scaled, rt, *value_grads = probs(comp_len, queries, grads, *keys, own_keys)
    value_back = y_return(value_grads[:4])
    d_query, *key_grads = slopes(queries, scaled, rt, p, *keys, own_keys, *values, own_values)
    key_grads[4], *value_back = lax.optimization_barrier((key_grads[4], *value_back))
    key_back = y_return(key_grads[:4])
    operands = (comp_len, rt, p, *values, own_values)
    half = rows(0, (), *operands)
    value_parts = z_exchange(sum_segments(value_back))
    *key_back, half = lax.optimization_barrier((*key_back, half))
    key_sum, value_parts = lax.optimization_barrier((sum_segments(key_back), value_parts))
    key_parts = z_exchange(key_sum)
    value_blocks = x_spread(z_sum(value_parts))
    out = rows(1, (half,), *operands)
    key_parts, out, *value_blocks = lax.optimization_barrier((key_parts, out, *value_blocks))
    key_block, _ = core_pick(x_spread(z_sum(key_parts)), owner_route)
    value_block, _ = core_pick(value_blocks, owner_route)

    d_own = jnp.stack([key_grads[4], value_grads[4]], axis=1)
    d_prompt = jnp.stack([key_block, value_block], axis=1)
    return out[None], d_query[None], d_own[None], d_prompt[None]


def solution(mesh):
    fine = Mesh(mesh.devices.reshape(2, 4, 4, 2, 4), ("z_hi", "y", "x", "core", "z_lo"))
    samples, group, rows = ("z_hi", "y", "x", "core"), ("x", "core"), ("z_hi", "y", "z_lo")
    in_specs = (
        P(samples, None, "z_lo"),
        P(samples, None, None, "z_lo"),
        P(group, rows, None, None),
        P(samples, None, "z_lo"),
        P(),
        P(samples),
    )
    out_specs = (
        P(samples, None, "z_lo"),
        P(samples, None, "z_lo"),
        P(samples, None, None, "z_lo"),
        P(group, rows, None, None),
    )
    return jax.shard_map(local, mesh=fine, in_specs=in_specs, out_specs=out_specs, check_vma=False)
```

time: 157 us -> 146 us (0.930)
  between operations: 12 us -> 5.63 us
  Pallas kernels: 44 us -> 40.5 us
  starting transfers between devices: 63.7 us -> 65.3 us
    pallas_call x2 -> x3, Pallas kernels: 30.3 us -> 26.9 us  [the longest x1 15.5 us: local(): slopes(queries, scaled, rt, p, *keys, own_keys, *values, own_values)]
    ppermute x28, starting transfers between devices: 44.5 us -> 46.4 us  [shift(): return lax.ppermute(x, axis, [(i, (i + by) % size) for i in range(size)])]
    all_to_all x4, waiting for transfers between devices: 16.7 us -> 15.1 us  [z_exchange(): return lax.all_to_all(parts, ('z_hi', 'z_lo'), 0, 0, tiled=True)]
    unnamed x26 -> x28, local copies, waits for them, and re-layouts: 3.69 us -> 3.69 us
  transfers between devices with their start and end apart: 32 -> 32, of which waited for: 8 -> 7; matrix products, arithmetic and copies ran while one was open for 6% -> 6% of each run, Pallas kernels for 28% -> 28%
where the time goes in v1:
time: 146 us
  starting transfers between devices  65.3 us (45%)
  Pallas kernels  40.5 us (28%)
  waiting for transfers between devices  21 us (14%)
  local copies, waits for them, and re-layouts  8.78 us (6%)
  between operations  5.63 us (4%)
  other arithmetic  4.4 us (3%)
    ppermute x28, starting transfers between devices, shift(): return lax.ppermute(x, axis, [(i, (i + by) % size) for i in range(size)])  46.4 us
    all_to_all x4, starting transfers between devices, z_exchange(): return lax.all_to_all(parts, ('z_hi', 'z_lo'), 0, 0, tiled=True)  18.9 us
    pallas_call x1, Pallas kernels, local(): slopes(queries, scaled, rt, p, *keys, own_keys, *values, own_values)  15.5 us
    all_to_all x4, waiting for transfers between devices, z_exchange(): return lax.all_to_all(parts, ('z_hi', 'z_lo'), 0, 0, tiled=True)  15.1 us
    pallas_call x1, Pallas kernels, local(): probs(comp_len, queries, grads, *keys, own_keys)  13.7 us
    pallas_call x2, Pallas kernels, rows(): pl.pallas_call(lambda *refs: rows_kernel(half * RATIO, *refs), grid_spec=...  11.4 us
    ppermute x28, waiting for transfers between devices, shift(): return lax.ppermute(x, axis, [(i, (i + by) % size) for i in range(size)])  5.88 us
    unnamed x28, local copies, waits for them, and re-layouts  3.69 us
  transfers between devices with their start and end apart: 32, of which 7 were waited for; matrix products, arithmetic and copies ran while one was open for 6% of the time, Pallas kernels for 28%

profile of v1, /device:TPU:1, one launch (start us, length us, event | category | flops | bytes accessed | tf_op | source)
XLA Modules:
  0.0 145.6 jit_solution(6465430756591117510)
XLA Ops:
  0.6 1.5 %fusion.5 = (bf16[1,64,1,1024]{3,2,1,0:T(2,128)(2,1)S(1)}, bf16[1,64,1,1024]{3,2,1,0:T(2,128)(2,1)S(1)}) fusion(bf16[1,64,2,1024]{3,2,1,0:T(2,128)(2,1)} %param.8), kind=kLoop, calls=%fused_computation.29 | loop fusion | bytes 524288 | tf_op jit(solution)/shard_map/slice | solution.py:318
  2.2 3.7 %collective-permute-start.1 = (bf16[64,1024]{1,0:T(8,128)(2,1)S(1)}, bf16[64,1024]{1,0:T(8,128)(2,1)S(1)}, u32[]{:S(2)}, u32[]{:S(2)}) collective-permute-start(bf16[64,1024]{1,0:T(8,128)(2,1)S(1)} %bitcast.91), channel_id=1, source_target_pairs={{0,16},{8,24},{16,0},{24,8},{1,17},{9,25},{17,1},{25,9},{2,18},{10... | collective-permute-start | bytes 393224 | tf_op jit(solution)/shard_map/ppermute | solution.py:246
  5.8 0.9 collective-permute-start.2
  6.7 0.6 collective-permute-start
  7.3 0.8 select_reduce_fusion
  8.1 1.3 fusion.6
  10.1 1.7 %collective-permute-done.2 = bf16[64,1024]{1,0:T(8,128)(2,1)S(1)} collective-permute-done((bf16[64,1024]{1,0:T(8,128)(2,1)S(1)}, bf16[64,1024]{1,0:T(8,128)(2,1)S(1)}, u32[]{:S(2)}, u32[]{:S(2)}) %collective-permute-start.2) | collective-permute-done | bytes 131104 | tf_op jit(solution)/shard_map/ppermute | solution.py:246
  11.8 2.2 %collective-permute-done = bf16[64,1024]{1,0:T(8,128)(2,1)S(1)} collective-permute-done((bf16[64,1024]{1,0:T(8,128)(2,1)S(1)}, bf16[64,1024]{1,0:T(8,128)(2,1)S(1)}, u32[]{:S(2)}, u32[]{:S(2)}) %collective-permute-start) | collective-permute-done | bytes 131104 | tf_op jit(solution)/shard_map/ppermute | solution.py:246
  14.1 1.1 collective-permute-start.3
  16.5 0.9 collective-permute-start.6
  17.3 0.5 collective-permute-start.5
  17.9 0.6 collective-permute-start.4
  18.6 0.7 pad_maximum_fusion
  19.3 8.2 %all-to-all-start = ((bf16[8,64,256]{2,1,0:T(8,128)(2,1)}), bf16[8,64,256]{2,1,0:T(8,128)(2,1)S(1)}, u32[]{:S(2)}, u32[]{:S(2)}) async-start(bf16[8,64,256]{2,1,0:T(8,128)(2,1)} %pad_maximum_fusion), calls=%async_computation | async-start | bytes 524288 | tf_op jit(solution)/shard_map/all_to_all | solution.py:279
  27.5 1.2 collective-permute-start.7
  28.7 1.0 collective-permute-done.7
  29.8 7.9 %all-to-all-done = bf16[8,64,256]{2,1,0:T(8,128)(2,1)S(1)} async-done(((bf16[8,64,256]{2,1,0:T(8,128)(2,1)}), bf16[8,64,256]{2,1,0:T(8,128)(2,1)S(1)}, u32[]{:S(2)}, u32[]{:S(2)}) %all-to-all-start) | async-done | bytes 262176 | tf_op jit(solution)/shard_map/all_to_all | solution.py:279
  37.7 2.7 %collective-permute-start.10 = (bf16[512,256]{1,0:T(8,128)(2,1)S(1)}, bf16[512,256]{1,0:T(8,128)(2,1)S(1)}, u32[]{:S(2)}, u32[]{:S(2)}) collective-permute-start(bf16[512,256]{1,0:T(8,128)(2,1)S(1)} %bitcast.86), channel_id=1, source_target_pairs={{0,96},{32,0},{64,32},{96,64},{1,97},{33,1},{65,33},{97,65},{2,98}... | collective-permute-start | bytes 786440 | tf_op jit(solution)/shard_map/ppermute | solution.py:246
  40.8 0.7 collective-permute-start.8
  41.5 0.7 pad_maximum_fusion.1
  42.2 3.4 %all-to-all-start.1 = ((bf16[8,64,256]{2,1,0:T(8,128)(2,1)}), bf16[8,64,256]{2,1,0:T(8,128)(2,1)S(1)}, u32[]{:S(2)}, u32[]{:S(2)}) async-start(bf16[8,64,256]{2,1,0:T(8,128)(2,1)} %pad_maximum_fusion.1), calls=%async_computation.1 | async-start | bytes 524288 | tf_op jit(solution)/shard_map/all_to_all | solution.py:279
  45.6 1.5 %fusion.4 = (bf16[1,256,1,256]{3,2,1,0:T(2,128)(2,1)S(1)}, bf16[1,256,1,256]{3,2,1,0:T(2,128)(2,1)S(1)}) fusion(bf16[1,256,2,256]{3,2,1,0:T(2,128)(2,1)} %param.7), kind=kLoop, calls=%fused_computation.28 | loop fusion | bytes 524288 | tf_op jit(solution)/shard_map/slice | solution.py:310
  49.7 0.8 copy_bitcast_fusion
  50.5 4.5 %all-to-all-done.1 = bf16[8,64,256]{2,1,0:T(8,128)(2,1)S(1)} async-done(((bf16[8,64,256]{2,1,0:T(8,128)(2,1)}), bf16[8,64,256]{2,1,0:T(8,128)(2,1)S(1)}, u32[]{:S(2)}, u32[]{:S(2)}) %all-to-all-start.1) | async-done | bytes 262176 | tf_op jit(solution)/shard_map/all_to_all | solution.py:279
  54.9 2.0 %collective-permute-start.13 = (bf16[512,256]{1,0:T(8,128)(2,1)S(1)}, bf16[512,256]{1,0:T(8,128)(2,1)S(1)}, u32[]{:S(2)}, u32[]{:S(2)}) collective-permute-start(bf16[512,256]{1,0:T(8,128)(2,1)S(1)} %bitcast.61), channel_id=1, source_target_pairs={{0,96},{32,0},{64,32},{96,64},{1,97},{33,1},{65,33},{97,65},{2,98}... | collective-permute-start | bytes 786440 | tf_op jit(solution)/shard_map/ppermute | solution.py:246
  56.9 1.4 collective-permute-start.12
  58.4 0.6 copy-done.9
  59.2 13.7 %probs.1 = (bf16[10,2304,256]{2,1,0:T(8,128)(2,1)}, bf16[256,1280]{1,0:T(8,128)(2,1)}, f32[10,8,256]{2,1,0:T(8,128)}, bf16[512,256]{1,0:T(8,128)(2,1)}, bf16[512...) custom-call(s32[1]{0:T(128)S(6)} %copy.63.len_ref.refs_0_, ...), custom_call_target="tpu_custom_call" | custom-call | flops 6039797760 | bytes 20971520 | tf_op jit(solution)/shard_map/probs/pallas_call | solution.py:328
  72.9 2.7 %collective-permute-start.17 = (bf16[512,256]{1,0:T(8,128)(2,1)}, bf16[512,256]{1,0:T(8,128)(2,1)S(1)}, u32[]{:S(2)}, u32[]{:S(2)}) collective-permute-start(bf16[512,256]{1,0:T(8,128)(2,1)} %get-tuple-element.66), channel_id=1, source_target_pairs={{0,96},{32,0},{64,32},{96,64},{1,97},{33,1},{65,33},{97,65},{2,98}... | collective-permute-start | bytes 786440 | tf_op jit(solution)/shard_map/ppermute | solution.py:246
  77.1 15.5 %slopes.1 = (bf16[256,1280]{1,0:T(8,128)(2,1)}, bf16[512,256]{1,0:T(8,128)(2,1)}, bf16[512,256]{1,0:T(8,128)(2,1)}, bf16[512,256]{1,0:T(8,128)(2,1)}, bf16[512,2...) custom-call(bf16[256,1280]{1,0:T(8,128)(2,1)} %bitcast.98, bf16[256,1280]{1,0:T(8,128)(2,1)} %get-tuple-element.53.gs_ref, ...), custom_call_target="tpu_custom_call" | custom-call | flops 6039797760 | bytes 20971520 | tf_op jit(solution)/shard_map/slopes/pallas_call | solution.py:330
  92.6 2.4 %collective-permute-start.14 = (bf16[512,256]{1,0:T(8,128)(2,1)}, bf16[512,256]{1,0:T(8,128)(2,1)S(1)}, u32[]{:S(2)}, u32[]{:S(2)}) collective-permute-start(bf16[512,256]{1,0:T(8,128)(2,1)} %get-tuple-element.57), channel_id=1, source_target_pairs={{0,96},{32,0},{64,32},{96,64},{1,97},{33,1},{65,33},{97,65},{2,98}... | collective-permute-start | bytes 786440 | tf_op jit(solution)/shard_map/ppermute | solution.py:246
  95.1 1.4 collective-permute-start.15
  96.5 0.8 add_convert_fusion
  97.3 3.4 %all-to-all-start.2 = ((bf16[8,64,256]{2,1,0:T(8,128)(2,1)}), bf16[8,64,256]{2,1,0:T(8,128)(2,1)S(1)}, u32[]{:S(2)}, u32[]{:S(2)}) async-start(bf16[8,64,256]{2,1,0:T(8,128)(2,1)} %bitcast.17), calls=%async_computation.2 | async-start | bytes 524288 | tf_op jit(solution)/shard_map/all_to_all | solution.py:279
  100.8 5.7 %rows.2.refs_8_ = bf16[256,1280]{1,0:T(8,128)(2,1)} custom-call(s32[1]{0:T(128)S(6)} %copy.63.len_ref.refs_0_, f32[10,8,256]{2,1,0:T(8,128)} %get-tuple-element.54.rt_ref.refs_1_, bf16[10,2304,256]{2,1,0:T(8,128)(2,1)} %get-tuple-element.55.p_hbm.refs_2_, bf16[512,256]{1,0:T(8,128)(2,1)} %bitcast.65, bf16[512,256]{1,0:T(8,128)(2,1)} %copy-done.3, ...), custom_call_target="tpu_custom_call" | custom-call | flops 1 | bytes 1 | tf_op jit(solution)/shard_map/rows/pallas_call | solution.py:224
  106.5 0.8 add_convert_fusion.1
  107.3 2.7 %all-to-all-done.2 = bf16[8,64,256]{2,1,0:T(8,128)(2,1)S(1)} async-done(((bf16[8,64,256]{2,1,0:T(8,128)(2,1)}), bf16[8,64,256]{2,1,0:T(8,128)(2,1)S(1)}, u32[]{:S(2)}, u32[]{:S(2)}) %all-to-all-start.2) | async-done | bytes 262176 | tf_op jit(solution)/shard_map/all_to_all | solution.py:279
  110.0 3.9 %all-to-all-start.3 = ((bf16[8,64,256]{2,1,0:T(8,128)(2,1)}), bf16[8,64,256]{2,1,0:T(8,128)(2,1)S(1)}, u32[]{:S(2)}, u32[]{:S(2)}) async-start(bf16[8,64,256]{2,1,0:T(8,128)(2,1)} %bitcast.16), calls=%async_computation.3 | async-start | bytes 524288 | tf_op jit(solution)/shard_map/all_to_all | solution.py:279
  113.9 1.0 copy.38
  115.0 2.2 %collective-permute-start.22 = (bf16[64,1024]{1,0:T(8,128)(2,1)S(1)}, bf16[64,1024]{1,0:T(8,128)(2,1)S(1)}, u32[]{:S(2)}, u32[]{:S(2)}) collective-permute-start(bf16[64,1024]{1,0:T(8,128)(2,1)S(1)} %bitcast.72), channel_id=1, source_target_pairs={{0,24},{8,0},{16,8},{24,16},{1,25},{9,1},{17,9},{25,17},{2,26},{10... | collective-permute-start | bytes 393224 | tf_op jit(solution)/shard_map/ppermute | solution.py:246
  117.2 1.2 collective-permute-start.21
  118.4 5.7 %rows.3 = bf16[256,1280]{1,0:T(8,128)(2,1)} custom-call(s32[1]{0:T(128)S(6)} %copy.63.len_ref.refs_0_, f32[10,8,256]{2,1,0:T(8,128)} %get-tuple-element.54.rt_ref.refs_1_, bf16[10,2304,256]{2,1,0:T(8,128)(2,1)} %get-tuple-element.55.p_hbm.refs_2_, bf16[512,256]{1,0:T(8,128)(2,1)} %bitcast.66, ...), custom_call_target="tpu_custom_call", output_to_operand_aliasing={{}: (8, {})} | custom-call | flops 1509949440 | bytes 20971520 | tf_op jit(solution)/shard_map/rows/pallas_call | solution.py:224
  124.2 2.8 %collective-permute-start.25 = (bf16[64,1024]{1,0:T(8,128)(2,1)S(1)}, bf16[64,1024]{1,0:T(8,128)(2,1)S(1)}, u32[]{:S(2)}, u32[]{:S(2)}) collective-permute-start(bf16[64,1024]{1,0:T(8,128)(2,1)S(1)} %bitcast.77), channel_id=1, source_target_pairs={{0,24},{8,0},{16,8},{24,16},{1,25},{9,1},{17,9},{25,17},{2,26},{10... | collective-permute-start | bytes 393224 | tf_op jit(solution)/shard_map/ppermute | solution.py:246
  127.0 0.5 collective-permute-start.24
  127.7 11.0 %collective-permute-start.27 = (bf16[64,1024]{1,0:T(8,128)(2,1)S(1)}, bf16[64,1024]{1,0:T(8,128)(2,1)S(1)}, u32[]{:S(2)}, u32[]{:S(2)}) collective-permute-start(bf16[64,1024]{1,0:T(8,128)(2,1)S(1)} %select_select_fusion), channel_id=1, source_target_pairs={{0,4},{4,0},{1,5},{5,1},{2,6},{6,2},{3,7},{7,3},{8,12},{12,8},{9,1... | collective-permute-start | bytes 393224 | tf_op jit(solution)/shard_map/ppermute | solution.py:246
  138.8 4.8 %collective-permute-start.26 = (bf16[64,1024]{1,0:T(8,128)(2,1)S(1)}, bf16[64,1024]{1,0:T(8,128)(2,1)S(1)}, u32[]{:S(2)}, u32[]{:S(2)}) collective-permute-start(bf16[64,1024]{1,0:T(8,128)(2,1)S(1)} %select_select_fusion.1), channel_id=1, source_target_pairs={{0,4},{4,0},{1,5},{5,1},{2,6},{6,2},{3,7},{7,3},{8,12},{12,8},{9,1... | collective-permute-start | bytes 393224 | tf_op jit(solution)/shard_map/ppermute | solution.py:246
  143.6 0.9 collective-permute-done.26
  144.6 1.0 copy.39
  (75 shorter events, 2.9 us)
Async XLA Ops:
  2.2 7.9 %collective-permute-start.1 = (bf16[64,1024]{1,0:T(8,128)(2,1)S(1)}, bf16[64,1024]{1,0:T(8,128)(2,1)S(1)}, u32[]{:S(2)}, u32[]{:S(2)}) collective-permute-start(bf16[64,1024]{1,0:T(8,128)(2,1)S(1)} %bitcast.91), channel_id=1, source_target_pairs={{0,16},{8,24},{16,0},{24,8},{1,17},{9,25},{17,1},{25,9},{2,18},{10... | collective-permute-start | bytes 393224 | tf_op jit(solution)/shard_map/ppermute | solution.py:246
  5.8 6.0 %collective-permute-start.2 = (bf16[64,1024]{1,0:T(8,128)(2,1)S(1)}, bf16[64,1024]{1,0:T(8,128)(2,1)S(1)}, u32[]{:S(2)}, u32[]{:S(2)}) collective-permute-start(bf16[64,1024]{1,0:T(8,128)(2,1)S(1)} %bitcast.92), channel_id=1, source_target_pairs={{0,24},{8,0},{16,8},{24,16},{1,25},{9,1},{17,9},{25,17},{2,26},{10... | collective-permute-start | bytes 393224 | tf_op jit(solution)/shard_map/ppermute | solution.py:246
  6.7 7.3 %collective-permute-start = (bf16[64,1024]{1,0:T(8,128)(2,1)S(1)}, bf16[64,1024]{1,0:T(8,128)(2,1)S(1)}, u32[]{:S(2)}, u32[]{:S(2)}) collective-permute-start(bf16[64,1024]{1,0:T(8,128)(2,1)S(1)} %bitcast.93), channel_id=1, source_target_pairs={{0,8},{8,16},{16,24},{24,0},{1,9},{9,17},{17,25},{25,1},{2,10},{10... | collective-permute-start | bytes 393224 | tf_op jit(solution)/shard_map/ppermute | solution.py:246
  14.1 4.4 %collective-permute-start.3 = (bf16[64,1024]{1,0:T(8,128)(2,1)S(1)}, bf16[64,1024]{1,0:T(8,128)(2,1)S(1)}, u32[]{:S(2)}, u32[]{:S(2)}) collective-permute-start(bf16[64,1024]{1,0:T(8,128)(2,1)S(1)} %select_select_fusion.4), channel_id=1, source_target_pairs={{0,4},{4,0},{1,5},{5,1},{2,6},{6,2},{3,7},{7,3},{8,12},{12,8},{9,1... | collective-permute-start | bytes 393224 | tf_op jit(solution)/shard_map/ppermute | solution.py:246
  16.5 11.0 %collective-permute-start.6 = (bf16[64,1024]{1,0:T(8,128)(2,1)S(1)}, bf16[64,1024]{1,0:T(8,128)(2,1)S(1)}, u32[]{:S(2)}, u32[]{:S(2)}) collective-permute-start(bf16[64,1024]{1,0:T(8,128)(2,1)S(1)} %bitcast.67), channel_id=1, source_target_pairs={{0,24},{8,0},{16,8},{24,16},{1,25},{9,1},{17,9},{25,17},{2,26},{10... | collective-permute-start | bytes 393224 | tf_op jit(solution)/shard_map/ppermute | solution.py:246
  17.3 10.1 %collective-permute-start.5 = (bf16[64,1024]{1,0:T(8,128)(2,1)S(1)}, bf16[64,1024]{1,0:T(8,128)(2,1)S(1)}, u32[]{:S(2)}, u32[]{:S(2)}) collective-permute-start(bf16[64,1024]{1,0:T(8,128)(2,1)S(1)} %bitcast.68), channel_id=1, source_target_pairs={{0,16},{8,24},{16,0},{24,8},{1,17},{9,25},{17,1},{25,9},{2,18},{10... | collective-permute-start | bytes 393224 | tf_op jit(solution)/shard_map/ppermute | solution.py:246
  17.9 9.6 %collective-permute-start.4 = (bf16[64,1024]{1,0:T(8,128)(2,1)S(1)}, bf16[64,1024]{1,0:T(8,128)(2,1)S(1)}, u32[]{:S(2)}, u32[]{:S(2)}) collective-permute-start(bf16[64,1024]{1,0:T(8,128)(2,1)S(1)} %bitcast.69), channel_id=1, source_target_pairs={{0,8},{8,16},{16,24},{24,0},{1,9},{9,17},{17,25},{25,1},{2,10},{10... | collective-permute-start | bytes 393224 | tf_op jit(solution)/shard_map/ppermute | solution.py:246
  19.3 18.4 %all-to-all-start = ((bf16[8,64,256]{2,1,0:T(8,128)(2,1)}), bf16[8,64,256]{2,1,0:T(8,128)(2,1)S(1)}, u32[]{:S(2)}, u32[]{:S(2)}) async-start(bf16[8,64,256]{2,1,0:T(8,128)(2,1)} %pad_maximum_fusion), calls=%async_computation | async-start | bytes 524288 | tf_op jit(solution)/shard_map/all_to_all | solution.py:279
  27.5 2.2 %collective-permute-start.7 = (bf16[64,1024]{1,0:T(8,128)(2,1)S(1)}, bf16[64,1024]{1,0:T(8,128)(2,1)S(1)}, u32[]{:S(2)}, u32[]{:S(2)}) collective-permute-start(bf16[64,1024]{1,0:T(8,128)(2,1)S(1)} %select_select_fusion.2), channel_id=1, source_target_pairs={{0,4},{4,0},{1,5},{5,1},{2,6},{6,2},{3,7},{7,3},{8,12},{12,8},{9,1... | collective-permute-start | bytes 393224 | tf_op jit(solution)/shard_map/ppermute | solution.py:246
  37.7 20.7 %copy-start.6 = (bf16[8,64,256]{2,1,0:T(8,128)(2,1)}, bf16[8,64,256]{2,1,0:T(8,128)(2,1)S(1)}, u32[]{:S(2)}) copy-start(bf16[8,64,256]{2,1,0:T(8,128)(2,1)S(1)} %all-to-all-done) | copy-start | bytes 786436
  37.7 20.7 %collective-permute-start.10 = (bf16[512,256]{1,0:T(8,128)(2,1)S(1)}, bf16[512,256]{1,0:T(8,128)(2,1)S(1)}, u32[]{:S(2)}, u32[]{:S(2)}) collective-permute-start(bf16[512,256]{1,0:T(8,128)(2,1)S(1)} %bitcast.86), channel_id=1, source_target_pairs={{0,96},{32,0},{64,32},{96,64},{1,97},{33,1},{65,33},{97,65},{2,98}... | collective-permute-start | bytes 786440 | tf_op jit(solution)/shard_map/ppermute | solution.py:246
  40.4 18.0 %collective-permute-start.9 = (bf16[512,256]{1,0:T(8,128)(2,1)S(1)}, bf16[512,256]{1,0:T(8,128)(2,1)S(1)}, u32[]{:S(2)}, u32[]{:S(2)}) collective-permute-start(bf16[512,256]{1,0:T(8,128)(2,1)S(1)} %bitcast.87), channel_id=1, source_target_pairs={{0,64},{32,96},{64,0},{96,32},{1,65},{33,97},{65,1},{97,33},{2,66}... | collective-permute-start | bytes 786440 | tf_op jit(solution)/shard_map/ppermute | solution.py:246
  40.8 17.6 %collective-permute-start.8 = (bf16[512,256]{1,0:T(8,128)(2,1)S(1)}, bf16[512,256]{1,0:T(8,128)(2,1)S(1)}, u32[]{:S(2)}, u32[]{:S(2)}) collective-permute-start(bf16[512,256]{1,0:T(8,128)(2,1)S(1)} %bitcast.88), channel_id=1, source_target_pairs={{0,32},{32,64},{64,96},{96,0},{1,33},{33,65},{65,97},{97,1},{2,34}... | collective-permute-start | bytes 786440 | tf_op jit(solution)/shard_map/ppermute | solution.py:246
  42.2 12.8 %all-to-all-start.1 = ((bf16[8,64,256]{2,1,0:T(8,128)(2,1)}), bf16[8,64,256]{2,1,0:T(8,128)(2,1)S(1)}, u32[]{:S(2)}, u32[]{:S(2)}) async-start(bf16[8,64,256]{2,1,0:T(8,128)(2,1)} %pad_maximum_fusion.1), calls=%async_computation.1 | async-start | bytes 524288 | tf_op jit(solution)/shard_map/all_to_all | solution.py:279
  54.9 21.4 %copy-start = (bf16[8,64,256]{2,1,0:T(8,128)(2,1)}, bf16[8,64,256]{2,1,0:T(8,128)(2,1)S(1)}, u32[]{:S(2)}) copy-start(bf16[8,64,256]{2,1,0:T(8,128)(2,1)S(1)} %all-to-all-done.1) | copy-start | bytes 786436
  54.9 21.0 %collective-permute-start.13 = (bf16[512,256]{1,0:T(8,128)(2,1)S(1)}, bf16[512,256]{1,0:T(8,128)(2,1)S(1)}, u32[]{:S(2)}, u32[]{:S(2)}) collective-permute-start(bf16[512,256]{1,0:T(8,128)(2,1)S(1)} %bitcast.61), channel_id=1, source_target_pairs={{0,96},{32,0},{64,32},{96,64},{1,97},{33,1},{65,33},{97,65},{2,98}... | collective-permute-start | bytes 786440 | tf_op jit(solution)/shard_map/ppermute | solution.py:246
  56.9 19.3 %collective-permute-start.12 = (bf16[512,256]{1,0:T(8,128)(2,1)S(1)}, bf16[512,256]{1,0:T(8,128)(2,1)S(1)}, u32[]{:S(2)}, u32[]{:S(2)}) collective-permute-start(bf16[512,256]{1,0:T(8,128)(2,1)S(1)} %bitcast.62), channel_id=1, source_target_pairs={{0,64},{32,96},{64,0},{96,32},{1,65},{33,97},{65,1},{97,33},{2,66}... | collective-permute-start | bytes 786440 | tf_op jit(solution)/shard_map/ppermute | solution.py:246
  58.3 0.7 copy-start.9
  58.3 17.9 %collective-permute-start.11 = (bf16[512,256]{1,0:T(8,128)(2,1)S(1)}, bf16[512,256]{1,0:T(8,128)(2,1)S(1)}, u32[]{:S(2)}, u32[]{:S(2)}) collective-permute-start(bf16[512,256]{1,0:T(8,128)(2,1)S(1)} %bitcast.63), channel_id=1, source_target_pairs={{0,32},{32,64},{64,96},{96,0},{1,33},{33,65},{65,97},{97,1},{2,34}... | collective-permute-start | bytes 786440 | tf_op jit(solution)/shard_map/ppermute | solution.py:246
  58.4 0.8 copy-start.10
  58.4 0.8 copy-start.11
  72.9 23.6 %copy-start.4 = (bf16[512,256]{1,0:T(8,128)(2,1)S(1)}, bf16[512,256]{1,0:T(8,128)(2,1)}, u32[]{:S(2)}) copy-start(bf16[512,256]{1,0:T(8,128)(2,1)} %get-tuple-element.69) | copy-start | bytes 786436
  72.9 23.6 %collective-permute-start.17 = (bf16[512,256]{1,0:T(8,128)(2,1)}, bf16[512,256]{1,0:T(8,128)(2,1)S(1)}, u32[]{:S(2)}, u32[]{:S(2)}) collective-permute-start(bf16[512,256]{1,0:T(8,128)(2,1)} %get-tuple-element.66), channel_id=1, source_target_pairs={{0,96},{32,0},{64,32},{96,64},{1,97},{33,1},{65,33},{97,65},{2,98}... | collective-permute-start | bytes 786440 | tf_op jit(solution)/shard_map/ppermute | solution.py:246
  75.6 20.9 %collective-permute-start.18 = (bf16[512,256]{1,0:T(8,128)(2,1)}, bf16[512,256]{1,0:T(8,128)(2,1)S(1)}, u32[]{:S(2)}, u32[]{:S(2)}) collective-permute-start(bf16[512,256]{1,0:T(8,128)(2,1)} %get-tuple-element.67), channel_id=1, source_target_pairs={{0,64},{32,96},{64,0},{96,32},{1,65},{33,97},{65,1},{97,33},{2,66}... | collective-permute-start | bytes 786440 | tf_op jit(solution)/shard_map/ppermute | solution.py:246
  75.9 0.7 copy-start.1
  75.9 20.5 %collective-permute-start.19 = (bf16[512,256]{1,0:T(8,128)(2,1)}, bf16[512,256]{1,0:T(8,128)(2,1)S(1)}, u32[]{:S(2)}, u32[]{:S(2)}) collective-permute-start(bf16[512,256]{1,0:T(8,128)(2,1)} %get-tuple-element.68), channel_id=1, source_target_pairs={{0,32},{32,64},{64,96},{96,0},{1,33},{33,65},{65,97},{97,1},{2,34}... | collective-permute-start | bytes 786440 | tf_op jit(solution)/shard_map/ppermute | solution.py:246
  76.3 0.7 copy-start.2
  76.3 0.8 copy-start.3
  92.6 13.9 %copy-start.5 = (bf16[512,256]{1,0:T(8,128)(2,1)S(1)}, bf16[512,256]{1,0:T(8,128)(2,1)}, u32[]{:S(2)}) copy-start(bf16[512,256]{1,0:T(8,128)(2,1)} %get-tuple-element.60) | copy-start | bytes 786436
  92.6 21.3 %copy-start.7 = (bf16[256,256]{1,0:T(8,128)(2,1)S(1)}, bf16[256,256]{1,0:T(8,128)(2,1)}, u32[]{:S(2)}) copy-start(bf16[256,256]{1,0:T(8,128)(2,1)} %get-tuple-element.79) | copy-start | bytes 393220
  92.6 21.3 %copy-start.8 = (bf16[256,256]{1,0:T(8,128)(2,1)S(1)}, bf16[256,256]{1,0:T(8,128)(2,1)}, u32[]{:S(2)}) copy-start(bf16[256,256]{1,0:T(8,128)(2,1)} %get-tuple-element.78) | copy-start | bytes 393220
  92.6 13.8 %collective-permute-start.14 = (bf16[512,256]{1,0:T(8,128)(2,1)}, bf16[512,256]{1,0:T(8,128)(2,1)S(1)}, u32[]{:S(2)}, u32[]{:S(2)}) collective-permute-start(bf16[512,256]{1,0:T(8,128)(2,1)} %get-tuple-element.57), channel_id=1, source_target_pairs={{0,96},{32,0},{64,32},{96,64},{1,97},{33,1},{65,33},{97,65},{2,98}... | collective-permute-start | bytes 786440 | tf_op jit(solution)/shard_map/ppermute | solution.py:246
  95.1 11.4 %collective-permute-start.15 = (bf16[512,256]{1,0:T(8,128)(2,1)}, bf16[512,256]{1,0:T(8,128)(2,1)S(1)}, u32[]{:S(2)}, u32[]{:S(2)}) collective-permute-start(bf16[512,256]{1,0:T(8,128)(2,1)} %get-tuple-element.58), channel_id=1, source_target_pairs={{0,64},{32,96},{64,0},{96,32},{1,65},{33,97},{65,1},{97,33},{2,66}... | collective-permute-start | bytes 786440 | tf_op jit(solution)/shard_map/ppermute | solution.py:246
  96.5 10.0 %collective-permute-start.16 = (bf16[512,256]{1,0:T(8,128)(2,1)}, bf16[512,256]{1,0:T(8,128)(2,1)S(1)}, u32[]{:S(2)}, u32[]{:S(2)}) collective-permute-start(bf16[512,256]{1,0:T(8,128)(2,1)} %get-tuple-element.59), channel_id=1, source_target_pairs={{0,32},{32,64},{64,96},{96,0},{1,33},{33,65},{65,97},{97,1},{2,34}... | collective-permute-start | bytes 786440 | tf_op jit(solution)/shard_map/ppermute | solution.py:246
  97.3 12.7 %all-to-all-start.2 = ((bf16[8,64,256]{2,1,0:T(8,128)(2,1)}), bf16[8,64,256]{2,1,0:T(8,128)(2,1)S(1)}, u32[]{:S(2)}, u32[]{:S(2)}) async-start(bf16[8,64,256]{2,1,0:T(8,128)(2,1)} %bitcast.17), calls=%async_computation.2 | async-start | bytes 524288 | tf_op jit(solution)/shard_map/all_to_all | solution.py:279
  110.0 14.1 %all-to-all-start.3 = ((bf16[8,64,256]{2,1,0:T(8,128)(2,1)}), bf16[8,64,256]{2,1,0:T(8,128)(2,1)S(1)}, u32[]{:S(2)}, u32[]{:S(2)}) async-start(bf16[8,64,256]{2,1,0:T(8,128)(2,1)} %bitcast.16), calls=%async_computation.3 | async-start | bytes 524288 | tf_op jit(solution)/shard_map/all_to_all | solution.py:279
  115.0 9.1 %collective-permute-start.22 = (bf16[64,1024]{1,0:T(8,128)(2,1)S(1)}, bf16[64,1024]{1,0:T(8,128)(2,1)S(1)}, u32[]{:S(2)}, u32[]{:S(2)}) collective-permute-start(bf16[64,1024]{1,0:T(8,128)(2,1)S(1)} %bitcast.72), channel_id=1, source_target_pairs={{0,24},{8,0},{16,8},{24,16},{1,25},{9,1},{17,9},{25,17},{2,26},{10... | collective-permute-start | bytes 393224 | tf_op jit(solution)/shard_map/ppermute | solution.py:246
  117.2 6.9 %collective-permute-start.21 = (bf16[64,1024]{1,0:T(8,128)(2,1)S(1)}, bf16[64,1024]{1,0:T(8,128)(2,1)S(1)}, u32[]{:S(2)}, u32[]{:S(2)}) collective-permute-start(bf16[64,1024]{1,0:T(8,128)(2,1)S(1)} %bitcast.73), channel_id=1, source_target_pairs={{0,16},{8,24},{16,0},{24,8},{1,17},{9,25},{17,1},{25,9},{2,18},{10... | collective-permute-start | bytes 393224 | tf_op jit(solution)/shard_map/ppermute | solution.py:246
  118.4 5.7 %collective-permute-start.20 = (bf16[64,1024]{1,0:T(8,128)(2,1)S(1)}, bf16[64,1024]{1,0:T(8,128)(2,1)S(1)}, u32[]{:S(2)}, u32[]{:S(2)}) collective-permute-start(bf16[64,1024]{1,0:T(8,128)(2,1)S(1)} %bitcast.74), channel_id=1, source_target_pairs={{0,8},{8,16},{16,24},{24,0},{1,9},{9,17},{17,25},{25,1},{2,10},{10... | collective-permute-start | bytes 393224 | tf_op jit(solution)/shard_map/ppermute | solution.py:246
  124.2 14.5 %collective-permute-start.25 = (bf16[64,1024]{1,0:T(8,128)(2,1)S(1)}, bf16[64,1024]{1,0:T(8,128)(2,1)S(1)}, u32[]{:S(2)}, u32[]{:S(2)}) collective-permute-start(bf16[64,1024]{1,0:T(8,128)(2,1)S(1)} %bitcast.77), channel_id=1, source_target_pairs={{0,24},{8,0},{16,8},{24,16},{1,25},{9,1},{17,9},{25,17},{2,26},{10... | collective-permute-start | bytes 393224 | tf_op jit(solution)/shard_map/ppermute | solution.py:246
  127.0 11.7 %collective-permute-start.24 = (bf16[64,1024]{1,0:T(8,128)(2,1)S(1)}, bf16[64,1024]{1,0:T(8,128)(2,1)S(1)}, u32[]{:S(2)}, u32[]{:S(2)}) collective-permute-start(bf16[64,1024]{1,0:T(8,128)(2,1)S(1)} %bitcast.78), channel_id=1, source_target_pairs={{0,16},{8,24},{16,0},{24,8},{1,17},{9,25},{17,1},{25,9},{2,18},{10... | collective-permute-start | bytes 393224 | tf_op jit(solution)/shard_map/ppermute | solution.py:246
  127.5 11.2 %collective-permute-start.23 = (bf16[64,1024]{1,0:T(8,128)(2,1)S(1)}, bf16[64,1024]{1,0:T(8,128)(2,1)S(1)}, u32[]{:S(2)}, u32[]{:S(2)}) collective-permute-start(bf16[64,1024]{1,0:T(8,128)(2,1)S(1)} %bitcast.79), channel_id=1, source_target_pairs={{0,8},{8,16},{16,24},{24,0},{1,9},{9,17},{17,25},{25,1},{2,10},{10... | collective-permute-start | bytes 393224 | tf_op jit(solution)/shard_map/ppermute | solution.py:246
  127.7 15.9 %collective-permute-start.27 = (bf16[64,1024]{1,0:T(8,128)(2,1)S(1)}, bf16[64,1024]{1,0:T(8,128)(2,1)S(1)}, u32[]{:S(2)}, u32[]{:S(2)}) collective-permute-start(bf16[64,1024]{1,0:T(8,128)(2,1)S(1)} %select_select_fusion), channel_id=1, source_target_pairs={{0,4},{4,0},{1,5},{5,1},{2,6},{6,2},{3,7},{7,3},{8,12},{12,8},{9,1... | collective-permute-start | bytes 393224 | tf_op jit(solution)/shard_map/ppermute | solution.py:246
  138.8 5.8 %collective-permute-start.26 = (bf16[64,1024]{1,0:T(8,128)(2,1)S(1)}, bf16[64,1024]{1,0:T(8,128)(2,1)S(1)}, u32[]{:S(2)}, u32[]{:S(2)}) collective-permute-start(bf16[64,1024]{1,0:T(8,128)(2,1)S(1)} %select_select_fusion.1), channel_id=1, source_target_pairs={{0,4},{4,0},{1,5},{5,1},{2,6},{6,2},{3,7},{7,3},{8,12},{12,8},{9,1... | collective-permute-start | bytes 393224 | tf_op jit(solution)/shard_map/ppermute | solution.py:246

commit v2 on v1

--- a/solution.py
+++ b/solution.py
@@ -111,24 +111,29 @@
 def slopes_kernel(q_ref, gs_ref, rt_ref, p_hbm, k0, k1, k2, k3, ko, v0, v1, v2, v3, vo, dq_ref, d0, d1, d2, d3, do, f_ref, p_ref, sl_ref, acc_ref, kt_ref, sems):
     base = pl.program_id(0) * RATIO
     tiles = tiles_of((v0, v1, v2, v3, vo))
-    deltas, fetches = {}, []
-    for r in range(RATIO):
-        fetch = pltpu.make_async_copy(p_hbm.at[base + r], p_ref.at[r], sems.at[r])
-        fetch.start()
-        fetches.append(fetch)
+    deltas = {}
+
+    def fetch(r):
+        return pltpu.make_async_copy(p_hbm.at[r], p_ref.at[r], sems.at[r])
+
+    @pl.when(base == 0)
+    def _():
+        for r in range(2 * RATIO):
+            fetch(r).start()
+
     for ref, start, row in tiles_of((k0, k1, k2, k3, ko)):
         kt_ref[:, row : row + TILE] = ref[start : start + TILE, :].T
 
     def flow(r, ref, start, row):
         f = dot_nt(ref[start : start + TILE, :], gs_ref[:, r * HEAD : (r + 1) * HEAD])
         f_ref[r % 2, row : row + TILE, :] = f
-        part = fold(f * p_ref[r, row : row + TILE, :].astype(F32), jnp.sum)
+        part = fold(f * p_ref[base + r, row : row + TILE, :].astype(F32), jnp.sum)
         deltas[r] = deltas[r] + part if r in deltas else part
 
     for step in range(RATIO + 2):
         now, last, older = step, step - 1, step - 2
         if now < RATIO:
-            fetches[now].wait()
+            fetch(base + now).wait()
         if 0 <= last < RATIO:
             delta = jnp.sum(deltas[last], axis=0, keepdims=True) * rt_ref[last, 0:1, :]
             qt = q_ref[:, last * HEAD : (last + 1) * HEAD].T
@@ -139,7 +144,7 @@
             if now < RATIO:
                 flow(now, ref, start, row)
             if 0 <= last < RATIO:
-                p = p_ref[last, row : row + TILE, :].astype(F32)
+                p = p_ref[base + last, row : row + TILE, :].astype(F32)
                 sl = (p * (f_ref[last % 2, row : row + TILE, :] - delta)).astype(BF16)
                 sl_ref[last % 2, row : row + TILE, :] = sl
                 add_to(acc_ref, row, dot_nt(qt, sl), last == 0)
@@ -207,11 +212,11 @@
         out_specs=[five_spec] + seg_specs,
         scratch_shapes=[
             score_planes,
-            five_planes,
+            pltpu.VMEM((count, keys, ROWS), BF16),
             pltpu.VMEM((2, keys, ROWS), BF16),
             sums,
             pltpu.VMEM((HEAD, keys), BF16),
-            sems,
+            pltpu.SemaphoreType.DMA((count,)),
         ],
         out_shape=[head_shape] + seg_shapes,
         compiler_params=params,
@@ -319,11 +324,11 @@
     key_block, value_block = core_pick(x_spread(key_block), prompt_route, value_block)
     key_segment = z_gather(key_block)
     value_block, _ = core_pick(x_spread(value_block), prompt_route)
-    key_segment, value_block = lax.optimization_barrier((key_segment, value_block))
+    key_segment, value_block, owner_route = lax.optimization_barrier((key_segment, value_block, owner_route))
     keys = y_gather(key_segment)
     value_segment = z_gather(value_block)
     values = y_gather(value_segment)
-    queries, value_segment, owner_route = lax.optimization_barrier((queries, value_segment, owner_route))
+    queries, value_segment = lax.optimization_barrier((queries, value_segment))
 
     p, scaled, rt, *value_grads = probs(comp_len, queries, grads, *keys, own_keys)
     value_back = y_return(value_grads[:4])
@@ -337,9 +342,11 @@
     key_sum, value_parts = lax.optimization_barrier((sum_segments(key_back), value_parts))
     key_parts = z_exchange(key_sum)
     value_blocks = x_spread(z_sum(value_parts))
+    key_parts, *value_blocks = lax.optimization_barrier((key_parts, *value_blocks))
+    key_blocks = x_spread(z_sum(key_parts))
     out = rows(1, (half,), *operands)
-    key_parts, out, *value_blocks = lax.optimization_barrier((key_parts, out, *value_blocks))
-    key_block, _ = core_pick(x_spread(z_sum(key_parts)), owner_route)
+    out, *key_blocks = lax.optimization_barrier((out, *key_blocks))
+    key_block, _ = core_pick(key_blocks, owner_route)
     value_block, _ = core_pick(value_blocks, owner_route)
 
     d_own = jnp.stack([key_grads[4], value_grads[4]], axis=1)

time: 146 us -> 145 us (level)
  transfers between devices with their start and end apart: 32 -> 32, of which waited for: 7 -> 6; matrix products, arithmetic and copies ran while one was open for 6% -> 6% of each run, Pallas kernels for 28% -> 27%
where the time goes in v2:
time: 145 us; the launch traced here: 144 us
  starting transfers between devices  65.3 us (45%)
  Pallas kernels  39.3 us (27%)
  waiting for transfers between devices  20.9 us (14%)
  local copies, waits for them, and re-layouts  8.78 us (6%)
  between operations  5.65 us (4%)
  other arithmetic  4.41 us (3%)
    ppermute x28, starting transfers between devices, shift(): return lax.ppermute(x, axis, [(i, (i + by) % size) for i in range(size)])  46.4 us
    all_to_all x4, starting transfers between devices, z_exchange(): return lax.all_to_all(parts, ('z_hi', 'z_lo'), 0, 0, tiled=True)  18.9 us
    all_to_all x4, waiting for transfers between devices, z_exchange(): return lax.all_to_all(parts, ('z_hi', 'z_lo'), 0, 0, tiled=True)  16 us
    pallas_call x1, Pallas kernels, local(): slopes(queries, scaled, rt, p, *keys, own_keys, *values, own_values)  14.3 us
    pallas_call x1, Pallas kernels, local(): probs(comp_len, queries, grads, *keys, own_keys)  13.7 us
    pallas_call x2, Pallas kernels, rows(): pl.pallas_call(lambda *refs: rows_kernel(half * RATIO, *refs), grid_spec=...  11.4 us
    ppermute x28, waiting for transfers between devices, shift(): return lax.ppermute(x, axis, [(i, (i + by) % size) for i in range(size)])  4.9 us
    unnamed x28, local copies, waits for them, and re-layouts  3.69 us
  transfers between devices with their start and end apart: 32, of which 6 were waited for; matrix products, arithmetic and copies ran while one was open for 6% of the time, Pallas kernels for 27%

profile of v2, /device:TPU:1, one launch (start us, length us, event | category | flops | bytes accessed | tf_op | source)
XLA Modules:
  0.0 144.4 jit_solution(10541838617821660361)
XLA Ops:
  0.6 1.5 %fusion.5 = (bf16[1,64,1,1024]{3,2,1,0:T(2,128)(2,1)S(1)}, bf16[1,64,1,1024]{3,2,1,0:T(2,128)(2,1)S(1)}) fusion(bf16[1,64,2,1024]{3,2,1,0:T(2,128)(2,1)} %param.8), kind=kLoop, calls=%fused_computation.29 | loop fusion | bytes 524288 | tf_op jit(solution)/shard_map/slice | solution.py:323
  2.2 3.7 %collective-permute-start.1 = (bf16[64,1024]{1,0:T(8,128)(2,1)S(1)}, bf16[64,1024]{1,0:T(8,128)(2,1)S(1)}, u32[]{:S(2)}, u32[]{:S(2)}) collective-permute-start(bf16[64,1024]{1,0:T(8,128)(2,1)S(1)} %bitcast.91), channel_id=1, source_target_pairs={{0,16},{8,24},{16,0},{24,8},{1,17},{9,25},{17,1},{25,9},{2,18},{10... | collective-permute-start | bytes 393224 | tf_op jit(solution)/shard_map/ppermute | solution.py:251
  5.8 0.9 collective-permute-start.2
  6.7 0.6 collective-permute-start
  7.3 0.8 select_reduce_fusion
  8.1 1.3 fusion.6
  10.1 1.7 %collective-permute-done.2 = bf16[64,1024]{1,0:T(8,128)(2,1)S(1)} collective-permute-done((bf16[64,1024]{1,0:T(8,128)(2,1)S(1)}, bf16[64,1024]{1,0:T(8,128)(2,1)S(1)}, u32[]{:S(2)}, u32[]{:S(2)}) %collective-permute-start.2) | collective-permute-done | bytes 131104 | tf_op jit(solution)/shard_map/ppermute | solution.py:251
  11.8 2.2 %collective-permute-done = bf16[64,1024]{1,0:T(8,128)(2,1)S(1)} collective-permute-done((bf16[64,1024]{1,0:T(8,128)(2,1)S(1)}, bf16[64,1024]{1,0:T(8,128)(2,1)S(1)}, u32[]{:S(2)}, u32[]{:S(2)}) %collective-permute-start) | collective-permute-done | bytes 131104 | tf_op jit(solution)/shard_map/ppermute | solution.py:251
  14.1 1.1 collective-permute-start.3
  16.5 0.9 collective-permute-start.6
  17.3 0.5 collective-permute-start.5
  17.9 0.6 collective-permute-start.4
  18.6 0.7 pad_maximum_fusion
  19.3 8.2 %all-to-all-start = ((bf16[8,64,256]{2,1,0:T(8,128)(2,1)}), bf16[8,64,256]{2,1,0:T(8,128)(2,1)S(1)}, u32[]{:S(2)}, u32[]{:S(2)}) async-start(bf16[8,64,256]{2,1,0:T(8,128)(2,1)} %pad_maximum_fusion), calls=%async_computation | async-start | bytes 524288 | tf_op jit(solution)/shard_map/all_to_all | solution.py:284
  27.5 1.2 collective-permute-start.7
  30.8 6.9 %all-to-all-done = bf16[8,64,256]{2,1,0:T(8,128)(2,1)S(1)} async-done(((bf16[8,64,256]{2,1,0:T(8,128)(2,1)}), bf16[8,64,256]{2,1,0:T(8,128)(2,1)S(1)}, u32[]{:S(2)}, u32[]{:S(2)}) %all-to-all-start) | async-done | bytes 262176 | tf_op jit(solution)/shard_map/all_to_all | solution.py:284
  37.7 2.7 %collective-permute-start.10 = (bf16[512,256]{1,0:T(8,128)(2,1)S(1)}, bf16[512,256]{1,0:T(8,128)(2,1)S(1)}, u32[]{:S(2)}, u32[]{:S(2)}) collective-permute-start(bf16[512,256]{1,0:T(8,128)(2,1)S(1)} %bitcast.86), channel_id=1, source_target_pairs={{0,96},{32,0},{64,32},{96,64},{1,97},{33,1},{65,33},{97,65},{2,98}... | collective-permute-start | bytes 786440 | tf_op jit(solution)/shard_map/ppermute | solution.py:251
  40.8 0.7 collective-permute-start.8
  41.5 0.7 pad_maximum_fusion.1
  42.2 3.4 %all-to-all-start.1 = ((bf16[8,64,256]{2,1,0:T(8,128)(2,1)}), bf16[8,64,256]{2,1,0:T(8,128)(2,1)S(1)}, u32[]{:S(2)}, u32[]{:S(2)}) async-start(bf16[8,64,256]{2,1,0:T(8,128)(2,1)} %pad_maximum_fusion.1), calls=%async_computation.1 | async-start | bytes 524288 | tf_op jit(solution)/shard_map/all_to_all | solution.py:284
  45.6 1.5 %fusion.4 = (bf16[1,256,1,256]{3,2,1,0:T(2,128)(2,1)S(1)}, bf16[1,256,1,256]{3,2,1,0:T(2,128)(2,1)S(1)}) fusion(bf16[1,256,2,256]{3,2,1,0:T(2,128)(2,1)} %param.7), kind=kLoop, calls=%fused_computation.28 | loop fusion | bytes 524288 | tf_op jit(solution)/shard_map/slice | solution.py:315
  47.7 0.8 copy_bitcast_fusion
  48.5 6.5 %all-to-all-done.1 = bf16[8,64,256]{2,1,0:T(8,128)(2,1)S(1)} async-done(((bf16[8,64,256]{2,1,0:T(8,128)(2,1)}), bf16[8,64,256]{2,1,0:T(8,128)(2,1)S(1)}, u32[]{:S(2)}, u32[]{:S(2)}) %all-to-all-start.1) | async-done | bytes 262176 | tf_op jit(solution)/shard_map/all_to_all | solution.py:284
  54.9 2.0 %collective-permute-start.13 = (bf16[512,256]{1,0:T(8,128)(2,1)S(1)}, bf16[512,256]{1,0:T(8,128)(2,1)S(1)}, u32[]{:S(2)}, u32[]{:S(2)}) collective-permute-start(bf16[512,256]{1,0:T(8,128)(2,1)S(1)} %bitcast.61), channel_id=1, source_target_pairs={{0,96},{32,0},{64,32},{96,64},{1,97},{33,1},{65,33},{97,65},{2,98}... | collective-permute-start | bytes 786440 | tf_op jit(solution)/shard_map/ppermute | solution.py:251
  56.9 1.4 collective-permute-start.12
  58.4 0.6 copy-done.9
  59.2 13.7 %probs.1 = (bf16[10,2304,256]{2,1,0:T(8,128)(2,1)}, bf16[256,1280]{1,0:T(8,128)(2,1)}, f32[10,8,256]{2,1,0:T(8,128)}, bf16[512,256]{1,0:T(8,128)(2,1)}, bf16[512...) custom-call(s32[1]{0:T(128)S(6)} %copy.63.len_ref.refs_0_, ...), custom_call_target="tpu_custom_call" | custom-call | flops 6039797760 | bytes 20971520 | tf_op jit(solution)/shard_map/probs/pallas_call | solution.py:333
  72.9 2.7 %collective-permute-start.17 = (bf16[512,256]{1,0:T(8,128)(2,1)}, bf16[512,256]{1,0:T(8,128)(2,1)S(1)}, u32[]{:S(2)}, u32[]{:S(2)}) collective-permute-start(bf16[512,256]{1,0:T(8,128)(2,1)} %get-tuple-element.71), channel_id=1, source_target_pairs={{0,96},{32,0},{64,32},{96,64},{1,97},{33,1},{65,33},{97,65},{2,98}... | collective-permute-start | bytes 786440 | tf_op jit(solution)/shard_map/ppermute | solution.py:251
  76.3 0.4 copy-done.1
  77.1 14.3 %slopes.1 = (bf16[256,1280]{1,0:T(8,128)(2,1)}, bf16[512,256]{1,0:T(8,128)(2,1)}, bf16[512,256]{1,0:T(8,128)(2,1)}, bf16[512,256]{1,0:T(8,128)(2,1)}, bf16[512,2...) custom-call(bf16[256,1280]{1,0:T(8,128)(2,1)} %bitcast.98, bf16[256,1280]{1,0:T(8,128)(2,1)} %get-tuple-element.59.gs_ref, ...), custom_call_target="tpu_custom_call" | custom-call | flops 6039797760 | bytes 20971520 | tf_op jit(solution)/shard_map/slopes/pallas_call | solution.py:335
  91.4 2.4 %collective-permute-start.14 = (bf16[512,256]{1,0:T(8,128)(2,1)}, bf16[512,256]{1,0:T(8,128)(2,1)S(1)}, u32[]{:S(2)}, u32[]{:S(2)}) collective-permute-start(bf16[512,256]{1,0:T(8,128)(2,1)} %get-tuple-element.61), channel_id=1, source_target_pairs={{0,96},{32,0},{64,32},{96,64},{1,97},{33,1},{65,33},{97,65},{2,98}... | collective-permute-start | bytes 786440 | tf_op jit(solution)/shard_map/ppermute | solution.py:251
  93.9 1.4 collective-permute-start.15
  95.3 0.8 add_convert_fusion
  96.1 3.4 %all-to-all-start.2 = ((bf16[8,64,256]{2,1,0:T(8,128)(2,1)}), bf16[8,64,256]{2,1,0:T(8,128)(2,1)S(1)}, u32[]{:S(2)}, u32[]{:S(2)}) async-start(bf16[8,64,256]{2,1,0:T(8,128)(2,1)} %bitcast.17), calls=%async_computation.2 | async-start | bytes 524288 | tf_op jit(solution)/shard_map/all_to_all | solution.py:284
  99.6 5.7 %rows.2.refs_8_ = bf16[256,1280]{1,0:T(8,128)(2,1)} custom-call(s32[1]{0:T(128)S(6)} %copy.63.len_ref.refs_0_, f32[10,8,256]{2,1,0:T(8,128)} %get-tuple-element.57.rt_ref.refs_1_, bf16[10,2304,256]{2,1,0:T(8,128)(2,1)} %get-tuple-element.58.p_hbm.refs_2_, bf16[512,256]{1,0:T(8,128)(2,1)} %bitcast.65, bf16[512,256]{1,0:T(8,128)(2,1)} %copy-done.3, ...), custom_call_target="tpu_custom_call" | custom-call | flops 1 | bytes 1 | tf_op jit(solution)/shard_map/rows/pallas_call | solution.py:229
  105.3 0.8 add_convert_fusion.1
  106.1 2.7 %all-to-all-done.2 = bf16[8,64,256]{2,1,0:T(8,128)(2,1)S(1)} async-done(((bf16[8,64,256]{2,1,0:T(8,128)(2,1)}), bf16[8,64,256]{2,1,0:T(8,128)(2,1)S(1)}, u32[]{:S(2)}, u32[]{:S(2)}) %all-to-all-start.2) | async-done | bytes 262176 | tf_op jit(solution)/shard_map/all_to_all | solution.py:284
  108.8 3.9 %all-to-all-start.3 = ((bf16[8,64,256]{2,1,0:T(8,128)(2,1)}), bf16[8,64,256]{2,1,0:T(8,128)(2,1)S(1)}, u32[]{:S(2)}, u32[]{:S(2)}) async-start(bf16[8,64,256]{2,1,0:T(8,128)(2,1)} %bitcast.16), calls=%async_computation.3 | async-start | bytes 524288 | tf_op jit(solution)/shard_map/all_to_all | solution.py:284
  112.7 1.0 copy.38
  113.8 2.2 %collective-permute-start.22 = (bf16[64,1024]{1,0:T(8,128)(2,1)S(1)}, bf16[64,1024]{1,0:T(8,128)(2,1)S(1)}, u32[]{:S(2)}, u32[]{:S(2)}) collective-permute-start(bf16[64,1024]{1,0:T(8,128)(2,1)S(1)} %bitcast.72), channel_id=1, source_target_pairs={{0,24},{8,0},{16,8},{24,16},{1,25},{9,1},{17,9},{25,17},{2,26},{10... | collective-permute-start | bytes 393224 | tf_op jit(solution)/shard_map/ppermute | solution.py:251
  116.0 1.2 collective-permute-start.21
  117.2 5.7 %rows.3 = bf16[256,1280]{1,0:T(8,128)(2,1)} custom-call(s32[1]{0:T(128)S(6)} %copy.63.len_ref.refs_0_, f32[10,8,256]{2,1,0:T(8,128)} %get-tuple-element.57.rt_ref.refs_1_, bf16[10,2304,256]{2,1,0:T(8,128)(2,1)} %get-tuple-element.58.p_hbm.refs_2_, bf16[512,256]{1,0:T(8,128)(2,1)} %bitcast.66, ...), custom_call_target="tpu_custom_call", output_to_operand_aliasing={{}: (8, {})} | custom-call | flops 1509949440 | bytes 20971520 | tf_op jit(solution)/shard_map/rows/pallas_call | solution.py:229
  123.0 2.8 %collective-permute-start.25 = (bf16[64,1024]{1,0:T(8,128)(2,1)S(1)}, bf16[64,1024]{1,0:T(8,128)(2,1)S(1)}, u32[]{:S(2)}, u32[]{:S(2)}) collective-permute-start(bf16[64,1024]{1,0:T(8,128)(2,1)S(1)} %bitcast.77), channel_id=1, source_target_pairs={{0,24},{8,0},{16,8},{24,16},{1,25},{9,1},{17,9},{25,17},{2,26},{10... | collective-permute-start | bytes 393224 | tf_op jit(solution)/shard_map/ppermute | solution.py:251
  125.8 0.5 collective-permute-start.24
  126.5 11.0 %collective-permute-start.27 = (bf16[64,1024]{1,0:T(8,128)(2,1)S(1)}, bf16[64,1024]{1,0:T(8,128)(2,1)S(1)}, u32[]{:S(2)}, u32[]{:S(2)}) collective-permute-start(bf16[64,1024]{1,0:T(8,128)(2,1)S(1)} %select_select_fusion), channel_id=1, source_target_pairs={{0,4},{4,0},{1,5},{5,1},{2,6},{6,2},{3,7},{7,3},{8,12},{12,8},{9,1... | collective-permute-start | bytes 393224 | tf_op jit(solution)/shard_map/ppermute | solution.py:251
  137.5 4.8 %collective-permute-start.26 = (bf16[64,1024]{1,0:T(8,128)(2,1)S(1)}, bf16[64,1024]{1,0:T(8,128)(2,1)S(1)}, u32[]{:S(2)}, u32[]{:S(2)}) collective-permute-start(bf16[64,1024]{1,0:T(8,128)(2,1)S(1)} %select_select_fusion.1), channel_id=1, source_target_pairs={{0,4},{4,0},{1,5},{5,1},{2,6},{6,2},{3,7},{7,3},{8,12},{12,8},{9,1... | collective-permute-start | bytes 393224 | tf_op jit(solution)/shard_map/ppermute | solution.py:251
  142.4 0.9 collective-permute-done.26
  143.4 1.0 copy.39
  (75 shorter events, 2.6 us)
Async XLA Ops:
  2.2 7.9 %collective-permute-start.1 = (bf16[64,1024]{1,0:T(8,128)(2,1)S(1)}, bf16[64,1024]{1,0:T(8,128)(2,1)S(1)}, u32[]{:S(2)}, u32[]{:S(2)}) collective-permute-start(bf16[64,1024]{1,0:T(8,128)(2,1)S(1)} %bitcast.91), channel_id=1, source_target_pairs={{0,16},{8,24},{16,0},{24,8},{1,17},{9,25},{17,1},{25,9},{2,18},{10... | collective-permute-start | bytes 393224 | tf_op jit(solution)/shard_map/ppermute | solution.py:251
  5.8 6.0 %collective-permute-start.2 = (bf16[64,1024]{1,0:T(8,128)(2,1)S(1)}, bf16[64,1024]{1,0:T(8,128)(2,1)S(1)}, u32[]{:S(2)}, u32[]{:S(2)}) collective-permute-start(bf16[64,1024]{1,0:T(8,128)(2,1)S(1)} %bitcast.92), channel_id=1, source_target_pairs={{0,24},{8,0},{16,8},{24,16},{1,25},{9,1},{17,9},{25,17},{2,26},{10... | collective-permute-start | bytes 393224 | tf_op jit(solution)/shard_map/ppermute | solution.py:251
  6.7 7.3 %collective-permute-start = (bf16[64,1024]{1,0:T(8,128)(2,1)S(1)}, bf16[64,1024]{1,0:T(8,128)(2,1)S(1)}, u32[]{:S(2)}, u32[]{:S(2)}) collective-permute-start(bf16[64,1024]{1,0:T(8,128)(2,1)S(1)} %bitcast.93), channel_id=1, source_target_pairs={{0,8},{8,16},{16,24},{24,0},{1,9},{9,17},{17,25},{25,1},{2,10},{10... | collective-permute-start | bytes 393224 | tf_op jit(solution)/shard_map/ppermute | solution.py:251
  14.1 4.4 %collective-permute-start.3 = (bf16[64,1024]{1,0:T(8,128)(2,1)S(1)}, bf16[64,1024]{1,0:T(8,128)(2,1)S(1)}, u32[]{:S(2)}, u32[]{:S(2)}) collective-permute-start(bf16[64,1024]{1,0:T(8,128)(2,1)S(1)} %select_select_fusion.4), channel_id=1, source_target_pairs={{0,4},{4,0},{1,5},{5,1},{2,6},{6,2},{3,7},{7,3},{8,12},{12,8},{9,1... | collective-permute-start | bytes 393224 | tf_op jit(solution)/shard_map/ppermute | solution.py:251
  16.5 11.0 %collective-permute-start.6 = (bf16[64,1024]{1,0:T(8,128)(2,1)S(1)}, bf16[64,1024]{1,0:T(8,128)(2,1)S(1)}, u32[]{:S(2)}, u32[]{:S(2)}) collective-permute-start(bf16[64,1024]{1,0:T(8,128)(2,1)S(1)} %bitcast.67), channel_id=1, source_target_pairs={{0,24},{8,0},{16,8},{24,16},{1,25},{9,1},{17,9},{25,17},{2,26},{10... | collective-permute-start | bytes 393224 | tf_op jit(solution)/shard_map/ppermute | solution.py:251
  17.3 10.1 %collective-permute-start.5 = (bf16[64,1024]{1,0:T(8,128)(2,1)S(1)}, bf16[64,1024]{1,0:T(8,128)(2,1)S(1)}, u32[]{:S(2)}, u32[]{:S(2)}) collective-permute-start(bf16[64,1024]{1,0:T(8,128)(2,1)S(1)} %bitcast.68), channel_id=1, source_target_pairs={{0,16},{8,24},{16,0},{24,8},{1,17},{9,25},{17,1},{25,9},{2,18},{10... | collective-permute-start | bytes 393224 | tf_op jit(solution)/shard_map/ppermute | solution.py:251
  17.9 9.6 %collective-permute-start.4 = (bf16[64,1024]{1,0:T(8,128)(2,1)S(1)}, bf16[64,1024]{1,0:T(8,128)(2,1)S(1)}, u32[]{:S(2)}, u32[]{:S(2)}) collective-permute-start(bf16[64,1024]{1,0:T(8,128)(2,1)S(1)} %bitcast.69), channel_id=1, source_target_pairs={{0,8},{8,16},{16,24},{24,0},{1,9},{9,17},{17,25},{25,1},{2,10},{10... | collective-permute-start | bytes 393224 | tf_op jit(solution)/shard_map/ppermute | solution.py:251
  19.3 18.4 %all-to-all-start = ((bf16[8,64,256]{2,1,0:T(8,128)(2,1)}), bf16[8,64,256]{2,1,0:T(8,128)(2,1)S(1)}, u32[]{:S(2)}, u32[]{:S(2)}) async-start(bf16[8,64,256]{2,1,0:T(8,128)(2,1)} %pad_maximum_fusion), calls=%async_computation | async-start | bytes 524288 | tf_op jit(solution)/shard_map/all_to_all | solution.py:284
  27.5 3.2 %collective-permute-start.7 = (bf16[64,1024]{1,0:T(8,128)(2,1)S(1)}, bf16[64,1024]{1,0:T(8,128)(2,1)S(1)}, u32[]{:S(2)}, u32[]{:S(2)}) collective-permute-start(bf16[64,1024]{1,0:T(8,128)(2,1)S(1)} %select_select_fusion.2), channel_id=1, source_target_pairs={{0,4},{4,0},{1,5},{5,1},{2,6},{6,2},{3,7},{7,3},{8,12},{12,8},{9,1... | collective-permute-start | bytes 393224 | tf_op jit(solution)/shard_map/ppermute | solution.py:251
  37.7 20.7 %copy-start.6 = (bf16[8,64,256]{2,1,0:T(8,128)(2,1)}, bf16[8,64,256]{2,1,0:T(8,128)(2,1)S(1)}, u32[]{:S(2)}) copy-start(bf16[8,64,256]{2,1,0:T(8,128)(2,1)S(1)} %all-to-all-done) | copy-start | bytes 786436
  37.7 20.7 %collective-permute-start.10 = (bf16[512,256]{1,0:T(8,128)(2,1)S(1)}, bf16[512,256]{1,0:T(8,128)(2,1)S(1)}, u32[]{:S(2)}, u32[]{:S(2)}) collective-permute-start(bf16[512,256]{1,0:T(8,128)(2,1)S(1)} %bitcast.86), channel_id=1, source_target_pairs={{0,96},{32,0},{64,32},{96,64},{1,97},{33,1},{65,33},{97,65},{2,98}... | collective-permute-start | bytes 786440 | tf_op jit(solution)/shard_map/ppermute | solution.py:251
  40.4 18.0 %collective-permute-start.9 = (bf16[512,256]{1,0:T(8,128)(2,1)S(1)}, bf16[512,256]{1,0:T(8,128)(2,1)S(1)}, u32[]{:S(2)}, u32[]{:S(2)}) collective-permute-start(bf16[512,256]{1,0:T(8,128)(2,1)S(1)} %bitcast.87), channel_id=1, source_target_pairs={{0,64},{32,96},{64,0},{96,32},{1,65},{33,97},{65,1},{97,33},{2,66}... | collective-permute-start | bytes 786440 | tf_op jit(solution)/shard_map/ppermute | solution.py:251
  40.8 17.6 %collective-permute-start.8 = (bf16[512,256]{1,0:T(8,128)(2,1)S(1)}, bf16[512,256]{1,0:T(8,128)(2,1)S(1)}, u32[]{:S(2)}, u32[]{:S(2)}) collective-permute-start(bf16[512,256]{1,0:T(8,128)(2,1)S(1)} %bitcast.88), channel_id=1, source_target_pairs={{0,32},{32,64},{64,96},{96,0},{1,33},{33,65},{65,97},{97,1},{2,34}... | collective-permute-start | bytes 786440 | tf_op jit(solution)/shard_map/ppermute | solution.py:251
  42.2 12.8 %all-to-all-start.1 = ((bf16[8,64,256]{2,1,0:T(8,128)(2,1)}), bf16[8,64,256]{2,1,0:T(8,128)(2,1)S(1)}, u32[]{:S(2)}, u32[]{:S(2)}) async-start(bf16[8,64,256]{2,1,0:T(8,128)(2,1)} %pad_maximum_fusion.1), calls=%async_computation.1 | async-start | bytes 524288 | tf_op jit(solution)/shard_map/all_to_all | solution.py:284
  54.9 21.4 %copy-start = (bf16[8,64,256]{2,1,0:T(8,128)(2,1)}, bf16[8,64,256]{2,1,0:T(8,128)(2,1)S(1)}, u32[]{:S(2)}) copy-start(bf16[8,64,256]{2,1,0:T(8,128)(2,1)S(1)} %all-to-all-done.1) | copy-start | bytes 786436
  54.9 21.0 %collective-permute-start.13 = (bf16[512,256]{1,0:T(8,128)(2,1)S(1)}, bf16[512,256]{1,0:T(8,128)(2,1)S(1)}, u32[]{:S(2)}, u32[]{:S(2)}) collective-permute-start(bf16[512,256]{1,0:T(8,128)(2,1)S(1)} %bitcast.61), channel_id=1, source_target_pairs={{0,96},{32,0},{64,32},{96,64},{1,97},{33,1},{65,33},{97,65},{2,98}... | collective-permute-start | bytes 786440 | tf_op jit(solution)/shard_map/ppermute | solution.py:251
  56.9 19.3 %collective-permute-start.12 = (bf16[512,256]{1,0:T(8,128)(2,1)S(1)}, bf16[512,256]{1,0:T(8,128)(2,1)S(1)}, u32[]{:S(2)}, u32[]{:S(2)}) collective-permute-start(bf16[512,256]{1,0:T(8,128)(2,1)S(1)} %bitcast.62), channel_id=1, source_target_pairs={{0,64},{32,96},{64,0},{96,32},{1,65},{33,97},{65,1},{97,33},{2,66}... | collective-permute-start | bytes 786440 | tf_op jit(solution)/shard_map/ppermute | solution.py:251
  58.3 0.7 copy-start.9
  58.3 17.9 %collective-permute-start.11 = (bf16[512,256]{1,0:T(8,128)(2,1)S(1)}, bf16[512,256]{1,0:T(8,128)(2,1)S(1)}, u32[]{:S(2)}, u32[]{:S(2)}) collective-permute-start(bf16[512,256]{1,0:T(8,128)(2,1)S(1)} %bitcast.63), channel_id=1, source_target_pairs={{0,32},{32,64},{64,96},{96,0},{1,33},{33,65},{65,97},{97,1},{2,34}... | collective-permute-start | bytes 786440 | tf_op jit(solution)/shard_map/ppermute | solution.py:251
  58.4 0.8 copy-start.10
  58.4 0.8 copy-start.11
  72.9 22.4 %copy-start.4 = (bf16[512,256]{1,0:T(8,128)(2,1)S(1)}, bf16[512,256]{1,0:T(8,128)(2,1)}, u32[]{:S(2)}) copy-start(bf16[512,256]{1,0:T(8,128)(2,1)} %get-tuple-element.74) | copy-start | bytes 786436
  72.9 22.4 %collective-permute-start.17 = (bf16[512,256]{1,0:T(8,128)(2,1)}, bf16[512,256]{1,0:T(8,128)(2,1)S(1)}, u32[]{:S(2)}, u32[]{:S(2)}) collective-permute-start(bf16[512,256]{1,0:T(8,128)(2,1)} %get-tuple-element.71), channel_id=1, source_target_pairs={{0,96},{32,0},{64,32},{96,64},{1,97},{33,1},{65,33},{97,65},{2,98}... | collective-permute-start | bytes 786440 | tf_op jit(solution)/shard_map/ppermute | solution.py:251
  75.6 19.7 %collective-permute-start.18 = (bf16[512,256]{1,0:T(8,128)(2,1)}, bf16[512,256]{1,0:T(8,128)(2,1)S(1)}, u32[]{:S(2)}, u32[]{:S(2)}) collective-permute-start(bf16[512,256]{1,0:T(8,128)(2,1)} %get-tuple-element.72), channel_id=1, source_target_pairs={{0,64},{32,96},{64,0},{96,32},{1,65},{33,97},{65,1},{97,33},{2,66}... | collective-permute-start | bytes 786440 | tf_op jit(solution)/shard_map/ppermute | solution.py:251
  75.9 0.7 copy-start.1
  75.9 19.3 %collective-permute-start.19 = (bf16[512,256]{1,0:T(8,128)(2,1)}, bf16[512,256]{1,0:T(8,128)(2,1)S(1)}, u32[]{:S(2)}, u32[]{:S(2)}) collective-permute-start(bf16[512,256]{1,0:T(8,128)(2,1)} %get-tuple-element.73), channel_id=1, source_target_pairs={{0,32},{32,64},{64,96},{96,0},{1,33},{33,65},{65,97},{97,1},{2,34}... | collective-permute-start | bytes 786440 | tf_op jit(solution)/shard_map/ppermute | solution.py:251
  76.3 0.7 copy-start.2
  76.3 0.8 copy-start.3
  91.4 13.9 %copy-start.5 = (bf16[512,256]{1,0:T(8,128)(2,1)S(1)}, bf16[512,256]{1,0:T(8,128)(2,1)}, u32[]{:S(2)}) copy-start(bf16[512,256]{1,0:T(8,128)(2,1)} %get-tuple-element.65) | copy-start | bytes 786436
  91.4 21.3 %copy-start.7 = (bf16[256,256]{1,0:T(8,128)(2,1)S(1)}, bf16[256,256]{1,0:T(8,128)(2,1)}, u32[]{:S(2)}) copy-start(bf16[256,256]{1,0:T(8,128)(2,1)} %get-tuple-element.84) | copy-start | bytes 393220
  91.4 21.3 %copy-start.8 = (bf16[256,256]{1,0:T(8,128)(2,1)S(1)}, bf16[256,256]{1,0:T(8,128)(2,1)}, u32[]{:S(2)}) copy-start(bf16[256,256]{1,0:T(8,128)(2,1)} %get-tuple-element.83) | copy-start | bytes 393220
  91.4 13.8 %collective-permute-start.14 = (bf16[512,256]{1,0:T(8,128)(2,1)}, bf16[512,256]{1,0:T(8,128)(2,1)S(1)}, u32[]{:S(2)}, u32[]{:S(2)}) collective-permute-start(bf16[512,256]{1,0:T(8,128)(2,1)} %get-tuple-element.61), channel_id=1, source_target_pairs={{0,96},{32,0},{64,32},{96,64},{1,97},{33,1},{65,33},{97,65},{2,98}... | collective-permute-start | bytes 786440 | tf_op jit(solution)/shard_map/ppermute | solution.py:251
  93.9 11.4 %collective-permute-start.15 = (bf16[512,256]{1,0:T(8,128)(2,1)}, bf16[512,256]{1,0:T(8,128)(2,1)S(1)}, u32[]{:S(2)}, u32[]{:S(2)}) collective-permute-start(bf16[512,256]{1,0:T(8,128)(2,1)} %get-tuple-element.62), channel_id=1, source_target_pairs={{0,64},{32,96},{64,0},{96,32},{1,65},{33,97},{65,1},{97,33},{2,66}... | collective-permute-start | bytes 786440 | tf_op jit(solution)/shard_map/ppermute | solution.py:251
  95.3 10.0 %collective-permute-start.16 = (bf16[512,256]{1,0:T(8,128)(2,1)}, bf16[512,256]{1,0:T(8,128)(2,1)S(1)}, u32[]{:S(2)}, u32[]{:S(2)}) collective-permute-start(bf16[512,256]{1,0:T(8,128)(2,1)} %get-tuple-element.63), channel_id=1, source_target_pairs={{0,32},{32,64},{64,96},{96,0},{1,33},{33,65},{65,97},{97,1},{2,34}... | collective-permute-start | bytes 786440 | tf_op jit(solution)/shard_map/ppermute | solution.py:251
  96.1 12.7 %all-to-all-start.2 = ((bf16[8,64,256]{2,1,0:T(8,128)(2,1)}), bf16[8,64,256]{2,1,0:T(8,128)(2,1)S(1)}, u32[]{:S(2)}, u32[]{:S(2)}) async-start(bf16[8,64,256]{2,1,0:T(8,128)(2,1)} %bitcast.17), calls=%async_computation.2 | async-start | bytes 524288 | tf_op jit(solution)/shard_map/all_to_all | solution.py:284
  108.8 14.1 %all-to-all-start.3 = ((bf16[8,64,256]{2,1,0:T(8,128)(2,1)}), bf16[8,64,256]{2,1,0:T(8,128)(2,1)S(1)}, u32[]{:S(2)}, u32[]{:S(2)}) async-start(bf16[8,64,256]{2,1,0:T(8,128)(2,1)} %bitcast.16), calls=%async_computation.3 | async-start | bytes 524288 | tf_op jit(solution)/shard_map/all_to_all | solution.py:284
  113.8 9.1 %collective-permute-start.22 = (bf16[64,1024]{1,0:T(8,128)(2,1)S(1)}, bf16[64,1024]{1,0:T(8,128)(2,1)S(1)}, u32[]{:S(2)}, u32[]{:S(2)}) collective-permute-start(bf16[64,1024]{1,0:T(8,128)(2,1)S(1)} %bitcast.72), channel_id=1, source_target_pairs={{0,24},{8,0},{16,8},{24,16},{1,25},{9,1},{17,9},{25,17},{2,26},{10... | collective-permute-start | bytes 393224 | tf_op jit(solution)/shard_map/ppermute | solution.py:251
  116.0 6.9 %collective-permute-start.21 = (bf16[64,1024]{1,0:T(8,128)(2,1)S(1)}, bf16[64,1024]{1,0:T(8,128)(2,1)S(1)}, u32[]{:S(2)}, u32[]{:S(2)}) collective-permute-start(bf16[64,1024]{1,0:T(8,128)(2,1)S(1)} %bitcast.73), channel_id=1, source_target_pairs={{0,16},{8,24},{16,0},{24,8},{1,17},{9,25},{17,1},{25,9},{2,18},{10... | collective-permute-start | bytes 393224 | tf_op jit(solution)/shard_map/ppermute | solution.py:251
  117.2 5.7 %collective-permute-start.20 = (bf16[64,1024]{1,0:T(8,128)(2,1)S(1)}, bf16[64,1024]{1,0:T(8,128)(2,1)S(1)}, u32[]{:S(2)}, u32[]{:S(2)}) collective-permute-start(bf16[64,1024]{1,0:T(8,128)(2,1)S(1)} %bitcast.74), channel_id=1, source_target_pairs={{0,8},{8,16},{16,24},{24,0},{1,9},{9,17},{17,25},{25,1},{2,10},{10... | collective-permute-start | bytes 393224 | tf_op jit(solution)/shard_map/ppermute | solution.py:251
  123.0 14.5 %collective-permute-start.25 = (bf16[64,1024]{1,0:T(8,128)(2,1)S(1)}, bf16[64,1024]{1,0:T(8,128)(2,1)S(1)}, u32[]{:S(2)}, u32[]{:S(2)}) collective-permute-start(bf16[64,1024]{1,0:T(8,128)(2,1)S(1)} %bitcast.77), channel_id=1, source_target_pairs={{0,24},{8,0},{16,8},{24,16},{1,25},{9,1},{17,9},{25,17},{2,26},{10... | collective-permute-start | bytes 393224 | tf_op jit(solution)/shard_map/ppermute | solution.py:251
  125.8 11.7 %collective-permute-start.24 = (bf16[64,1024]{1,0:T(8,128)(2,1)S(1)}, bf16[64,1024]{1,0:T(8,128)(2,1)S(1)}, u32[]{:S(2)}, u32[]{:S(2)}) collective-permute-start(bf16[64,1024]{1,0:T(8,128)(2,1)S(1)} %bitcast.78), channel_id=1, source_target_pairs={{0,16},{8,24},{16,0},{24,8},{1,17},{9,25},{17,1},{25,9},{2,18},{10... | collective-permute-start | bytes 393224 | tf_op jit(solution)/shard_map/ppermute | solution.py:251
  126.3 11.2 %collective-permute-start.23 = (bf16[64,1024]{1,0:T(8,128)(2,1)S(1)}, bf16[64,1024]{1,0:T(8,128)(2,1)S(1)}, u32[]{:S(2)}, u32[]{:S(2)}) collective-permute-start(bf16[64,1024]{1,0:T(8,128)(2,1)S(1)} %bitcast.79), channel_id=1, source_target_pairs={{0,8},{8,16},{16,24},{24,0},{1,9},{9,17},{17,25},{25,1},{2,10},{10... | collective-permute-start | bytes 393224 | tf_op jit(solution)/shard_map/ppermute | solution.py:251
  126.5 15.9 %collective-permute-start.27 = (bf16[64,1024]{1,0:T(8,128)(2,1)S(1)}, bf16[64,1024]{1,0:T(8,128)(2,1)S(1)}, u32[]{:S(2)}, u32[]{:S(2)}) collective-permute-start(bf16[64,1024]{1,0:T(8,128)(2,1)S(1)} %select_select_fusion), channel_id=1, source_target_pairs={{0,4},{4,0},{1,5},{5,1},{2,6},{6,2},{3,7},{7,3},{8,12},{12,8},{9,1... | collective-permute-start | bytes 393224 | tf_op jit(solution)/shard_map/ppermute | solution.py:251
  137.5 5.8 %collective-permute-start.26 = (bf16[64,1024]{1,0:T(8,128)(2,1)S(1)}, bf16[64,1024]{1,0:T(8,128)(2,1)S(1)}, u32[]{:S(2)}, u32[]{:S(2)}) collective-permute-start(bf16[64,1024]{1,0:T(8,128)(2,1)S(1)} %select_select_fusion.1), channel_id=1, source_target_pairs={{0,4},{4,0},{1,5},{5,1},{2,6},{6,2},{3,7},{7,3},{8,12},{12,8},{9,1... | collective-permute-start | bytes 393224 | tf_op jit(solution)/shard_map/ppermute | solution.py:251

commit v3 on v2

--- a/solution.py
+++ b/solution.py
@@ -59,7 +59,10 @@
 def probs_kernel(len_ref, q_ref, g_ref, k0, k1, k2, k3, ko, p_hbm, gs_ref, rt_ref, d0, d1, d2, d3, do, s_ref, p_ref, acc_ref, sems):
     base = pl.program_id(0) * RATIO
     tiles = tiles_of((k0, k1, k2, k3, ko))
-    tops, totals, copies = {}, {}, []
+    tops, totals = {}, {}
+
+    def store(r):
+        return pltpu.make_async_copy(p_ref.at[r], p_hbm.at[r], sems.at[r])
 
     def score(r, ref, start, row):
         s = dot_nt(ref[start : start + TILE, :], q_ref[:, r * HEAD : (r + 1) * HEAD])
@@ -73,7 +76,7 @@
 
     def weigh(r, top, row):
         p = jnp.exp2(s_ref[r % 2, row : row + TILE, :] * LOG2 - top)
-        p_ref[r, row : row + TILE, :] = p.astype(BF16)
+        p_ref[base + r, row : row + TILE, :] = p.astype(BF16)
         part = fold(p, jnp.sum)
         totals[r] = totals[r] + part if r in totals else part
 
@@ -98,14 +101,15 @@
             if 0 <= last < RATIO:
                 weigh(last, top, row)
             if 0 <= older < RATIO:
-                add_to(acc_ref, row, dot_nt(gst, p_ref[older, row : row + TILE, :]), older == 0)
+                add_to(acc_ref, row, dot_nt(gst, p_ref[base + older, row : row + TILE, :]), older == 0)
         if 0 <= last < RATIO:
-            copy = pltpu.make_async_copy(p_ref.at[last], p_hbm.at[base + last], sems.at[last])
-            copy.start()
-            copies.append(copy)
+            store(base + last).start()
     store_segments((d0, d1, d2, d3, do), acc_ref, None)
-    for copy in copies:
-        copy.wait()
+
+    @pl.when(base > 0)
+    def _():
+        for r in range(2 * RATIO):
+            store(r).wait()
 
 
 def slopes_kernel(q_ref, gs_ref, rt_ref, p_hbm, k0, k1, k2, k3, ko, v0, v1, v2, v3, vo, dq_ref, d0, d1, d2, d3, do, f_ref, p_ref, sl_ref, acc_ref, kt_ref, sems):
@@ -198,7 +202,7 @@
             grid=(2,),
             in_specs=[five_spec, five_spec] + seg_specs,
             out_specs=[hbm, five_spec, five_rt] + seg_specs,
-            scratch_shapes=[score_planes, five_planes, sums, sems],
+            scratch_shapes=[score_planes, pltpu.VMEM((count, keys, ROWS), BF16), sums, pltpu.SemaphoreType.DMA((count,))],
         ),
         out_shape=[plane_shape, head_shape, rt_shape] + seg_shapes,
         compiler_params=params,

time: 145 us -> 145 us (level)
  no operation moved by 1% of the time
where the time goes in v3:
time: 145 us; the launch traced here: 144 us
  starting transfers between devices  65.3 us (45%)
  Pallas kernels  39.1 us (27%)
  waiting for transfers between devices  20.9 us (14%)
  local copies, waits for them, and re-layouts  8.78 us (6%)
  between operations  5.65 us (4%)
  other arithmetic  4.41 us (3%)
    ppermute x28, starting transfers between devices, shift(): return lax.ppermute(x, axis, [(i, (i + by) % size) for i in range(size)])  46.4 us
    all_to_all x4, starting transfers between devices, z_exchange(): return lax.all_to_all(parts, ('z_hi', 'z_lo'), 0, 0, tiled=True)  18.9 us
    all_to_all x4, waiting for transfers between devices, z_exchange(): return lax.all_to_all(parts, ('z_hi', 'z_lo'), 0, 0, tiled=True)  16 us
    pallas_call x1, Pallas kernels, local(): slopes(queries, scaled, rt, p, *keys, own_keys, *values, own_values)  14.3 us
    pallas_call x1, Pallas kernels, local(): probs(comp_len, queries, grads, *keys, own_keys)  13.4 us
    pallas_call x2, Pallas kernels, rows(): pl.pallas_call(lambda *refs: rows_kernel(half * RATIO, *refs), grid_spec=...  11.4 us
    ppermute x28, waiting for transfers between devices, shift(): return lax.ppermute(x, axis, [(i, (i + by) % size) for i in range(size)])  4.9 us
    unnamed x28, local copies, waits for them, and re-layouts  3.69 us
  transfers between devices with their start and end apart: 32, of which 6 were waited for; matrix products, arithmetic and copies ran while one was open for 6% of the time, Pallas kernels for 27%

profile of v3, /device:TPU:1, one launch (start us, length us, event | category | flops | bytes accessed | tf_op | source)
XLA Modules:
  0.0 144.1 jit_solution(13246714917624284064)
XLA Ops:
  0.6 1.5 %fusion.5 = (bf16[1,64,1,1024]{3,2,1,0:T(2,128)(2,1)S(1)}, bf16[1,64,1,1024]{3,2,1,0:T(2,128)(2,1)S(1)}) fusion(bf16[1,64,2,1024]{3,2,1,0:T(2,128)(2,1)} %param.8), kind=kLoop, calls=%fused_computation.29 | loop fusion | bytes 524288 | tf_op jit(solution)/shard_map/slice | solution.py:327
  2.2 3.7 %collective-permute-start.1 = (bf16[64,1024]{1,0:T(8,128)(2,1)S(1)}, bf16[64,1024]{1,0:T(8,128)(2,1)S(1)}, u32[]{:S(2)}, u32[]{:S(2)}) collective-permute-start(bf16[64,1024]{1,0:T(8,128)(2,1)S(1)} %bitcast.91), channel_id=1, source_target_pairs={{0,16},{8,24},{16,0},{24,8},{1,17},{9,25},{17,1},{25,9},{2,18},{10... | collective-permute-start | bytes 393224 | tf_op jit(solution)/shard_map/ppermute | solution.py:255
  5.8 0.9 collective-permute-start.2
  6.7 0.6 collective-permute-start
  7.3 0.8 select_reduce_fusion
  8.1 1.3 fusion.6
  10.1 1.7 %collective-permute-done.2 = bf16[64,1024]{1,0:T(8,128)(2,1)S(1)} collective-permute-done((bf16[64,1024]{1,0:T(8,128)(2,1)S(1)}, bf16[64,1024]{1,0:T(8,128)(2,1)S(1)}, u32[]{:S(2)}, u32[]{:S(2)}) %collective-permute-start.2) | collective-permute-done | bytes 131104 | tf_op jit(solution)/shard_map/ppermute | solution.py:255
  11.8 2.2 %collective-permute-done = bf16[64,1024]{1,0:T(8,128)(2,1)S(1)} collective-permute-done((bf16[64,1024]{1,0:T(8,128)(2,1)S(1)}, bf16[64,1024]{1,0:T(8,128)(2,1)S(1)}, u32[]{:S(2)}, u32[]{:S(2)}) %collective-permute-start) | collective-permute-done | bytes 131104 | tf_op jit(solution)/shard_map/ppermute | solution.py:255
  14.1 1.1 collective-permute-start.3
  16.5 0.9 collective-permute-start.6
  17.3 0.5 collective-permute-start.5
  17.9 0.6 collective-permute-start.4
  18.6 0.7 pad_maximum_fusion
  19.3 8.2 %all-to-all-start = ((bf16[8,64,256]{2,1,0:T(8,128)(2,1)}), bf16[8,64,256]{2,1,0:T(8,128)(2,1)S(1)}, u32[]{:S(2)}, u32[]{:S(2)}) async-start(bf16[8,64,256]{2,1,0:T(8,128)(2,1)} %pad_maximum_fusion), calls=%async_computation | async-start | bytes 524288 | tf_op jit(solution)/shard_map/all_to_all | solution.py:288
  27.5 1.2 collective-permute-start.7
  30.8 6.9 %all-to-all-done = bf16[8,64,256]{2,1,0:T(8,128)(2,1)S(1)} async-done(((bf16[8,64,256]{2,1,0:T(8,128)(2,1)}), bf16[8,64,256]{2,1,0:T(8,128)(2,1)S(1)}, u32[]{:S(2)}, u32[]{:S(2)}) %all-to-all-start) | async-done | bytes 262176 | tf_op jit(solution)/shard_map/all_to_all | solution.py:288
  37.7 2.7 %collective-permute-start.10 = (bf16[512,256]{1,0:T(8,128)(2,1)S(1)}, bf16[512,256]{1,0:T(8,128)(2,1)S(1)}, u32[]{:S(2)}, u32[]{:S(2)}) collective-permute-start(bf16[512,256]{1,0:T(8,128)(2,1)S(1)} %bitcast.86), channel_id=1, source_target_pairs={{0,96},{32,0},{64,32},{96,64},{1,97},{33,1},{65,33},{97,65},{2,98}... | collective-permute-start | bytes 786440 | tf_op jit(solution)/shard_map/ppermute | solution.py:255
  40.8 0.7 collective-permute-start.8
  41.5 0.7 pad_maximum_fusion.1
  42.2 3.4 %all-to-all-start.1 = ((bf16[8,64,256]{2,1,0:T(8,128)(2,1)}), bf16[8,64,256]{2,1,0:T(8,128)(2,1)S(1)}, u32[]{:S(2)}, u32[]{:S(2)}) async-start(bf16[8,64,256]{2,1,0:T(8,128)(2,1)} %pad_maximum_fusion.1), calls=%async_computation.1 | async-start | bytes 524288 | tf_op jit(solution)/shard_map/all_to_all | solution.py:288
  45.6 1.5 %fusion.4 = (bf16[1,256,1,256]{3,2,1,0:T(2,128)(2,1)S(1)}, bf16[1,256,1,256]{3,2,1,0:T(2,128)(2,1)S(1)}) fusion(bf16[1,256,2,256]{3,2,1,0:T(2,128)(2,1)} %param.7), kind=kLoop, calls=%fused_computation.28 | loop fusion | bytes 524288 | tf_op jit(solution)/shard_map/slice | solution.py:319
  47.7 0.8 copy_bitcast_fusion
  48.5 6.5 %all-to-all-done.1 = bf16[8,64,256]{2,1,0:T(8,128)(2,1)S(1)} async-done(((bf16[8,64,256]{2,1,0:T(8,128)(2,1)}), bf16[8,64,256]{2,1,0:T(8,128)(2,1)S(1)}, u32[]{:S(2)}, u32[]{:S(2)}) %all-to-all-start.1) | async-done | bytes 262176 | tf_op jit(solution)/shard_map/all_to_all | solution.py:288
  54.9 2.0 %collective-permute-start.13 = (bf16[512,256]{1,0:T(8,128)(2,1)S(1)}, bf16[512,256]{1,0:T(8,128)(2,1)S(1)}, u32[]{:S(2)}, u32[]{:S(2)}) collective-permute-start(bf16[512,256]{1,0:T(8,128)(2,1)S(1)} %bitcast.61), channel_id=1, source_target_pairs={{0,96},{32,0},{64,32},{96,64},{1,97},{33,1},{65,33},{97,65},{2,98}... | collective-permute-start | bytes 786440 | tf_op jit(solution)/shard_map/ppermute | solution.py:255
  56.9 1.4 collective-permute-start.12
  58.4 0.6 copy-done.9
  59.2 13.4 %probs.1 = (bf16[10,2304,256]{2,1,0:T(8,128)(2,1)}, bf16[256,1280]{1,0:T(8,128)(2,1)}, f32[10,8,256]{2,1,0:T(8,128)}, bf16[512,256]{1,0:T(8,128)(2,1)}, bf16[512...) custom-call(s32[1]{0:T(128)S(6)} %copy.63.len_ref.refs_0_, ...), custom_call_target="tpu_custom_call" | custom-call | flops 6039797760 | bytes 20971520 | tf_op jit(solution)/shard_map/probs/pallas_call | solution.py:337
  72.6 2.7 %collective-permute-start.17 = (bf16[512,256]{1,0:T(8,128)(2,1)}, bf16[512,256]{1,0:T(8,128)(2,1)S(1)}, u32[]{:S(2)}, u32[]{:S(2)}) collective-permute-start(bf16[512,256]{1,0:T(8,128)(2,1)} %get-tuple-element.71), channel_id=1, source_target_pairs={{0,96},{32,0},{64,32},{96,64},{1,97},{33,1},{65,33},{97,65},{2,98}... | collective-permute-start | bytes 786440 | tf_op jit(solution)/shard_map/ppermute | solution.py:255
  76.0 0.4 copy-done.1
  76.9 14.3 %slopes.1 = (bf16[256,1280]{1,0:T(8,128)(2,1)}, bf16[512,256]{1,0:T(8,128)(2,1)}, bf16[512,256]{1,0:T(8,128)(2,1)}, bf16[512,256]{1,0:T(8,128)(2,1)}, bf16[512,2...) custom-call(bf16[256,1280]{1,0:T(8,128)(2,1)} %bitcast.98, bf16[256,1280]{1,0:T(8,128)(2,1)} %get-tuple-element.59.gs_ref, ...), custom_call_target="tpu_custom_call" | custom-call | flops 6039797760 | bytes 20971520 | tf_op jit(solution)/shard_map/slopes/pallas_call | solution.py:339
  91.2 2.4 %collective-permute-start.14 = (bf16[512,256]{1,0:T(8,128)(2,1)}, bf16[512,256]{1,0:T(8,128)(2,1)S(1)}, u32[]{:S(2)}, u32[]{:S(2)}) collective-permute-start(bf16[512,256]{1,0:T(8,128)(2,1)} %get-tuple-element.61), channel_id=1, source_target_pairs={{0,96},{32,0},{64,32},{96,64},{1,97},{33,1},{65,33},{97,65},{2,98}... | collective-permute-start | bytes 786440 | tf_op jit(solution)/shard_map/ppermute | solution.py:255
  93.6 1.4 collective-permute-start.15
  95.1 0.8 add_convert_fusion
  95.9 3.4 %all-to-all-start.2 = ((bf16[8,64,256]{2,1,0:T(8,128)(2,1)}), bf16[8,64,256]{2,1,0:T(8,128)(2,1)S(1)}, u32[]{:S(2)}, u32[]{:S(2)}) async-start(bf16[8,64,256]{2,1,0:T(8,128)(2,1)} %bitcast.17), calls=%async_computation.2 | async-start | bytes 524288 | tf_op jit(solution)/shard_map/all_to_all | solution.py:288
  99.3 5.7 %rows.2.refs_8_ = bf16[256,1280]{1,0:T(8,128)(2,1)} custom-call(s32[1]{0:T(128)S(6)} %copy.63.len_ref.refs_0_, f32[10,8,256]{2,1,0:T(8,128)} %get-tuple-element.57.rt_ref.refs_1_, bf16[10,2304,256]{2,1,0:T(8,128)(2,1)} %get-tuple-element.58.p_hbm.refs_2_, bf16[512,256]{1,0:T(8,128)(2,1)} %bitcast.65, bf16[512,256]{1,0:T(8,128)(2,1)} %copy-done.3, ...), custom_call_target="tpu_custom_call" | custom-call | flops 1 | bytes 1 | tf_op jit(solution)/shard_map/rows/pallas_call | solution.py:233
  105.0 0.8 add_convert_fusion.1
  105.9 2.7 %all-to-all-done.2 = bf16[8,64,256]{2,1,0:T(8,128)(2,1)S(1)} async-done(((bf16[8,64,256]{2,1,0:T(8,128)(2,1)}), bf16[8,64,256]{2,1,0:T(8,128)(2,1)S(1)}, u32[]{:S(2)}, u32[]{:S(2)}) %all-to-all-start.2) | async-done | bytes 262176 | tf_op jit(solution)/shard_map/all_to_all | solution.py:288
  108.6 3.9 %all-to-all-start.3 = ((bf16[8,64,256]{2,1,0:T(8,128)(2,1)}), bf16[8,64,256]{2,1,0:T(8,128)(2,1)S(1)}, u32[]{:S(2)}, u32[]{:S(2)}) async-start(bf16[8,64,256]{2,1,0:T(8,128)(2,1)} %bitcast.16), calls=%async_computation.3 | async-start | bytes 524288 | tf_op jit(solution)/shard_map/all_to_all | solution.py:288
  112.5 1.0 copy.38
  113.6 2.2 %collective-permute-start.22 = (bf16[64,1024]{1,0:T(8,128)(2,1)S(1)}, bf16[64,1024]{1,0:T(8,128)(2,1)S(1)}, u32[]{:S(2)}, u32[]{:S(2)}) collective-permute-start(bf16[64,1024]{1,0:T(8,128)(2,1)S(1)} %bitcast.72), channel_id=1, source_target_pairs={{0,24},{8,0},{16,8},{24,16},{1,25},{9,1},{17,9},{25,17},{2,26},{10... | collective-permute-start | bytes 393224 | tf_op jit(solution)/shard_map/ppermute | solution.py:255
  115.7 1.2 collective-permute-start.21
  117.0 5.7 %rows.3 = bf16[256,1280]{1,0:T(8,128)(2,1)} custom-call(s32[1]{0:T(128)S(6)} %copy.63.len_ref.refs_0_, f32[10,8,256]{2,1,0:T(8,128)} %get-tuple-element.57.rt_ref.refs_1_, bf16[10,2304,256]{2,1,0:T(8,128)(2,1)} %get-tuple-element.58.p_hbm.refs_2_, bf16[512,256]{1,0:T(8,128)(2,1)} %bitcast.66, ...), custom_call_target="tpu_custom_call", output_to_operand_aliasing={{}: (8, {})} | custom-call | flops 1509949440 | bytes 20971520 | tf_op jit(solution)/shard_map/rows/pallas_call | solution.py:233
  122.8 2.8 %collective-permute-start.25 = (bf16[64,1024]{1,0:T(8,128)(2,1)S(1)}, bf16[64,1024]{1,0:T(8,128)(2,1)S(1)}, u32[]{:S(2)}, u32[]{:S(2)}) collective-permute-start(bf16[64,1024]{1,0:T(8,128)(2,1)S(1)} %bitcast.77), channel_id=1, source_target_pairs={{0,24},{8,0},{16,8},{24,16},{1,25},{9,1},{17,9},{25,17},{2,26},{10... | collective-permute-start | bytes 393224 | tf_op jit(solution)/shard_map/ppermute | solution.py:255
  125.5 0.5 collective-permute-start.24
  126.2 11.0 %collective-permute-start.27 = (bf16[64,1024]{1,0:T(8,128)(2,1)S(1)}, bf16[64,1024]{1,0:T(8,128)(2,1)S(1)}, u32[]{:S(2)}, u32[]{:S(2)}) collective-permute-start(bf16[64,1024]{1,0:T(8,128)(2,1)S(1)} %select_select_fusion), channel_id=1, source_target_pairs={{0,4},{4,0},{1,5},{5,1},{2,6},{6,2},{3,7},{7,3},{8,12},{12,8},{9,1... | collective-permute-start | bytes 393224 | tf_op jit(solution)/shard_map/ppermute | solution.py:255
  137.3 4.8 %collective-permute-start.26 = (bf16[64,1024]{1,0:T(8,128)(2,1)S(1)}, bf16[64,1024]{1,0:T(8,128)(2,1)S(1)}, u32[]{:S(2)}, u32[]{:S(2)}) collective-permute-start(bf16[64,1024]{1,0:T(8,128)(2,1)S(1)} %select_select_fusion.1), channel_id=1, source_target_pairs={{0,4},{4,0},{1,5},{5,1},{2,6},{6,2},{3,7},{7,3},{8,12},{12,8},{9,1... | collective-permute-start | bytes 393224 | tf_op jit(solution)/shard_map/ppermute | solution.py:255
  142.1 0.9 collective-permute-done.26
  143.2 1.0 copy.39
  (75 shorter events, 2.6 us)
Async XLA Ops:
  2.2 7.9 %collective-permute-start.1 = (bf16[64,1024]{1,0:T(8,128)(2,1)S(1)}, bf16[64,1024]{1,0:T(8,128)(2,1)S(1)}, u32[]{:S(2)}, u32[]{:S(2)}) collective-permute-start(bf16[64,1024]{1,0:T(8,128)(2,1)S(1)} %bitcast.91), channel_id=1, source_target_pairs={{0,16},{8,24},{16,0},{24,8},{1,17},{9,25},{17,1},{25,9},{2,18},{10... | collective-permute-start | bytes 393224 | tf_op jit(solution)/shard_map/ppermute | solution.py:255
  5.8 6.0 %collective-permute-start.2 = (bf16[64,1024]{1,0:T(8,128)(2,1)S(1)}, bf16[64,1024]{1,0:T(8,128)(2,1)S(1)}, u32[]{:S(2)}, u32[]{:S(2)}) collective-permute-start(bf16[64,1024]{1,0:T(8,128)(2,1)S(1)} %bitcast.92), channel_id=1, source_target_pairs={{0,24},{8,0},{16,8},{24,16},{1,25},{9,1},{17,9},{25,17},{2,26},{10... | collective-permute-start | bytes 393224 | tf_op jit(solution)/shard_map/ppermute | solution.py:255
  6.7 7.3 %collective-permute-start = (bf16[64,1024]{1,0:T(8,128)(2,1)S(1)}, bf16[64,1024]{1,0:T(8,128)(2,1)S(1)}, u32[]{:S(2)}, u32[]{:S(2)}) collective-permute-start(bf16[64,1024]{1,0:T(8,128)(2,1)S(1)} %bitcast.93), channel_id=1, source_target_pairs={{0,8},{8,16},{16,24},{24,0},{1,9},{9,17},{17,25},{25,1},{2,10},{10... | collective-permute-start | bytes 393224 | tf_op jit(solution)/shard_map/ppermute | solution.py:255
  14.1 4.4 %collective-permute-start.3 = (bf16[64,1024]{1,0:T(8,128)(2,1)S(1)}, bf16[64,1024]{1,0:T(8,128)(2,1)S(1)}, u32[]{:S(2)}, u32[]{:S(2)}) collective-permute-start(bf16[64,1024]{1,0:T(8,128)(2,1)S(1)} %select_select_fusion.4), channel_id=1, source_target_pairs={{0,4},{4,0},{1,5},{5,1},{2,6},{6,2},{3,7},{7,3},{8,12},{12,8},{9,1... | collective-permute-start | bytes 393224 | tf_op jit(solution)/shard_map/ppermute | solution.py:255
  16.5 11.0 %collective-permute-start.6 = (bf16[64,1024]{1,0:T(8,128)(2,1)S(1)}, bf16[64,1024]{1,0:T(8,128)(2,1)S(1)}, u32[]{:S(2)}, u32[]{:S(2)}) collective-permute-start(bf16[64,1024]{1,0:T(8,128)(2,1)S(1)} %bitcast.67), channel_id=1, source_target_pairs={{0,24},{8,0},{16,8},{24,16},{1,25},{9,1},{17,9},{25,17},{2,26},{10... | collective-permute-start | bytes 393224 | tf_op jit(solution)/shard_map/ppermute | solution.py:255
  17.3 10.1 %collective-permute-start.5 = (bf16[64,1024]{1,0:T(8,128)(2,1)S(1)}, bf16[64,1024]{1,0:T(8,128)(2,1)S(1)}, u32[]{:S(2)}, u32[]{:S(2)}) collective-permute-start(bf16[64,1024]{1,0:T(8,128)(2,1)S(1)} %bitcast.68), channel_id=1, source_target_pairs={{0,16},{8,24},{16,0},{24,8},{1,17},{9,25},{17,1},{25,9},{2,18},{10... | collective-permute-start | bytes 393224 | tf_op jit(solution)/shard_map/ppermute | solution.py:255
  17.9 9.6 %collective-permute-start.4 = (bf16[64,1024]{1,0:T(8,128)(2,1)S(1)}, bf16[64,1024]{1,0:T(8,128)(2,1)S(1)}, u32[]{:S(2)}, u32[]{:S(2)}) collective-permute-start(bf16[64,1024]{1,0:T(8,128)(2,1)S(1)} %bitcast.69), channel_id=1, source_target_pairs={{0,8},{8,16},{16,24},{24,0},{1,9},{9,17},{17,25},{25,1},{2,10},{10... | collective-permute-start | bytes 393224 | tf_op jit(solution)/shard_map/ppermute | solution.py:255
  19.3 18.4 %all-to-all-start = ((bf16[8,64,256]{2,1,0:T(8,128)(2,1)}), bf16[8,64,256]{2,1,0:T(8,128)(2,1)S(1)}, u32[]{:S(2)}, u32[]{:S(2)}) async-start(bf16[8,64,256]{2,1,0:T(8,128)(2,1)} %pad_maximum_fusion), calls=%async_computation | async-start | bytes 524288 | tf_op jit(solution)/shard_map/all_to_all | solution.py:288
  27.5 3.2 %collective-permute-start.7 = (bf16[64,1024]{1,0:T(8,128)(2,1)S(1)}, bf16[64,1024]{1,0:T(8,128)(2,1)S(1)}, u32[]{:S(2)}, u32[]{:S(2)}) collective-permute-start(bf16[64,1024]{1,0:T(8,128)(2,1)S(1)} %select_select_fusion.2), channel_id=1, source_target_pairs={{0,4},{4,0},{1,5},{5,1},{2,6},{6,2},{3,7},{7,3},{8,12},{12,8},{9,1... | collective-permute-start | bytes 393224 | tf_op jit(solution)/shard_map/ppermute | solution.py:255
  37.7 20.7 %copy-start.6 = (bf16[8,64,256]{2,1,0:T(8,128)(2,1)}, bf16[8,64,256]{2,1,0:T(8,128)(2,1)S(1)}, u32[]{:S(2)}) copy-start(bf16[8,64,256]{2,1,0:T(8,128)(2,1)S(1)} %all-to-all-done) | copy-start | bytes 786436
  37.7 20.7 %collective-permute-start.10 = (bf16[512,256]{1,0:T(8,128)(2,1)S(1)}, bf16[512,256]{1,0:T(8,128)(2,1)S(1)}, u32[]{:S(2)}, u32[]{:S(2)}) collective-permute-start(bf16[512,256]{1,0:T(8,128)(2,1)S(1)} %bitcast.86), channel_id=1, source_target_pairs={{0,96},{32,0},{64,32},{96,64},{1,97},{33,1},{65,33},{97,65},{2,98}... | collective-permute-start | bytes 786440 | tf_op jit(solution)/shard_map/ppermute | solution.py:255
  40.4 18.0 %collective-permute-start.9 = (bf16[512,256]{1,0:T(8,128)(2,1)S(1)}, bf16[512,256]{1,0:T(8,128)(2,1)S(1)}, u32[]{:S(2)}, u32[]{:S(2)}) collective-permute-start(bf16[512,256]{1,0:T(8,128)(2,1)S(1)} %bitcast.87), channel_id=1, source_target_pairs={{0,64},{32,96},{64,0},{96,32},{1,65},{33,97},{65,1},{97,33},{2,66}... | collective-permute-start | bytes 786440 | tf_op jit(solution)/shard_map/ppermute | solution.py:255
  40.8 17.6 %collective-permute-start.8 = (bf16[512,256]{1,0:T(8,128)(2,1)S(1)}, bf16[512,256]{1,0:T(8,128)(2,1)S(1)}, u32[]{:S(2)}, u32[]{:S(2)}) collective-permute-start(bf16[512,256]{1,0:T(8,128)(2,1)S(1)} %bitcast.88), channel_id=1, source_target_pairs={{0,32},{32,64},{64,96},{96,0},{1,33},{33,65},{65,97},{97,1},{2,34}... | collective-permute-start | bytes 786440 | tf_op jit(solution)/shard_map/ppermute | solution.py:255
  42.2 12.8 %all-to-all-start.1 = ((bf16[8,64,256]{2,1,0:T(8,128)(2,1)}), bf16[8,64,256]{2,1,0:T(8,128)(2,1)S(1)}, u32[]{:S(2)}, u32[]{:S(2)}) async-start(bf16[8,64,256]{2,1,0:T(8,128)(2,1)} %pad_maximum_fusion.1), calls=%async_computation.1 | async-start | bytes 524288 | tf_op jit(solution)/shard_map/all_to_all | solution.py:288
  54.9 21.1 %copy-start = (bf16[8,64,256]{2,1,0:T(8,128)(2,1)}, bf16[8,64,256]{2,1,0:T(8,128)(2,1)S(1)}, u32[]{:S(2)}) copy-start(bf16[8,64,256]{2,1,0:T(8,128)(2,1)S(1)} %all-to-all-done.1) | copy-start | bytes 786436
  54.9 20.7 %collective-permute-start.13 = (bf16[512,256]{1,0:T(8,128)(2,1)S(1)}, bf16[512,256]{1,0:T(8,128)(2,1)S(1)}, u32[]{:S(2)}, u32[]{:S(2)}) collective-permute-start(bf16[512,256]{1,0:T(8,128)(2,1)S(1)} %bitcast.61), channel_id=1, source_target_pairs={{0,96},{32,0},{64,32},{96,64},{1,97},{33,1},{65,33},{97,65},{2,98}... | collective-permute-start | bytes 786440 | tf_op jit(solution)/shard_map/ppermute | solution.py:255
  56.9 19.1 %collective-permute-start.12 = (bf16[512,256]{1,0:T(8,128)(2,1)S(1)}, bf16[512,256]{1,0:T(8,128)(2,1)S(1)}, u32[]{:S(2)}, u32[]{:S(2)}) collective-permute-start(bf16[512,256]{1,0:T(8,128)(2,1)S(1)} %bitcast.62), channel_id=1, source_target_pairs={{0,64},{32,96},{64,0},{96,32},{1,65},{33,97},{65,1},{97,33},{2,66}... | collective-permute-start | bytes 786440 | tf_op jit(solution)/shard_map/ppermute | solution.py:255
  58.3 0.7 copy-start.9
  58.3 17.7 %collective-permute-start.11 = (bf16[512,256]{1,0:T(8,128)(2,1)S(1)}, bf16[512,256]{1,0:T(8,128)(2,1)S(1)}, u32[]{:S(2)}, u32[]{:S(2)}) collective-permute-start(bf16[512,256]{1,0:T(8,128)(2,1)S(1)} %bitcast.63), channel_id=1, source_target_pairs={{0,32},{32,64},{64,96},{96,0},{1,33},{33,65},{65,97},{97,1},{2,34}... | collective-permute-start | bytes 786440 | tf_op jit(solution)/shard_map/ppermute | solution.py:255
  58.4 0.8 copy-start.10
  58.4 0.8 copy-start.11
  72.6 22.4 %copy-start.4 = (bf16[512,256]{1,0:T(8,128)(2,1)S(1)}, bf16[512,256]{1,0:T(8,128)(2,1)}, u32[]{:S(2)}) copy-start(bf16[512,256]{1,0:T(8,128)(2,1)} %get-tuple-element.74) | copy-start | bytes 786436
  72.6 22.4 %collective-permute-start.17 = (bf16[512,256]{1,0:T(8,128)(2,1)}, bf16[512,256]{1,0:T(8,128)(2,1)S(1)}, u32[]{:S(2)}, u32[]{:S(2)}) collective-permute-start(bf16[512,256]{1,0:T(8,128)(2,1)} %get-tuple-element.71), channel_id=1, source_target_pairs={{0,96},{32,0},{64,32},{96,64},{1,97},{33,1},{65,33},{97,65},{2,98}... | collective-permute-start | bytes 786440 | tf_op jit(solution)/shard_map/ppermute | solution.py:255
  75.3 19.7 %collective-permute-start.18 = (bf16[512,256]{1,0:T(8,128)(2,1)}, bf16[512,256]{1,0:T(8,128)(2,1)S(1)}, u32[]{:S(2)}, u32[]{:S(2)}) collective-permute-start(bf16[512,256]{1,0:T(8,128)(2,1)} %get-tuple-element.72), channel_id=1, source_target_pairs={{0,64},{32,96},{64,0},{96,32},{1,65},{33,97},{65,1},{97,33},{2,66}... | collective-permute-start | bytes 786440 | tf_op jit(solution)/shard_map/ppermute | solution.py:255
  75.7 0.7 copy-start.1
  75.7 19.4 %collective-permute-start.19 = (bf16[512,256]{1,0:T(8,128)(2,1)}, bf16[512,256]{1,0:T(8,128)(2,1)S(1)}, u32[]{:S(2)}, u32[]{:S(2)}) collective-permute-start(bf16[512,256]{1,0:T(8,128)(2,1)} %get-tuple-element.73), channel_id=1, source_target_pairs={{0,32},{32,64},{64,96},{96,0},{1,33},{33,65},{65,97},{97,1},{2,34}... | collective-permute-start | bytes 786440 | tf_op jit(solution)/shard_map/ppermute | solution.py:255
  76.0 0.7 copy-start.2
  76.0 0.8 copy-start.3
  91.2 13.9 %copy-start.5 = (bf16[512,256]{1,0:T(8,128)(2,1)S(1)}, bf16[512,256]{1,0:T(8,128)(2,1)}, u32[]{:S(2)}) copy-start(bf16[512,256]{1,0:T(8,128)(2,1)} %get-tuple-element.65) | copy-start | bytes 786436
  91.2 21.3 %copy-start.7 = (bf16[256,256]{1,0:T(8,128)(2,1)S(1)}, bf16[256,256]{1,0:T(8,128)(2,1)}, u32[]{:S(2)}) copy-start(bf16[256,256]{1,0:T(8,128)(2,1)} %get-tuple-element.84) | copy-start | bytes 393220
  91.2 21.3 %copy-start.8 = (bf16[256,256]{1,0:T(8,128)(2,1)S(1)}, bf16[256,256]{1,0:T(8,128)(2,1)}, u32[]{:S(2)}) copy-start(bf16[256,256]{1,0:T(8,128)(2,1)} %get-tuple-element.83) | copy-start | bytes 393220
  91.2 13.8 %collective-permute-start.14 = (bf16[512,256]{1,0:T(8,128)(2,1)}, bf16[512,256]{1,0:T(8,128)(2,1)S(1)}, u32[]{:S(2)}, u32[]{:S(2)}) collective-permute-start(bf16[512,256]{1,0:T(8,128)(2,1)} %get-tuple-element.61), channel_id=1, source_target_pairs={{0,96},{32,0},{64,32},{96,64},{1,97},{33,1},{65,33},{97,65},{2,98}... | collective-permute-start | bytes 786440 | tf_op jit(solution)/shard_map/ppermute | solution.py:255
  93.6 11.4 %collective-permute-start.15 = (bf16[512,256]{1,0:T(8,128)(2,1)}, bf16[512,256]{1,0:T(8,128)(2,1)S(1)}, u32[]{:S(2)}, u32[]{:S(2)}) collective-permute-start(bf16[512,256]{1,0:T(8,128)(2,1)} %get-tuple-element.62), channel_id=1, source_target_pairs={{0,64},{32,96},{64,0},{96,32},{1,65},{33,97},{65,1},{97,33},{2,66}... | collective-permute-start | bytes 786440 | tf_op jit(solution)/shard_map/ppermute | solution.py:255
  95.0 10.0 %collective-permute-start.16 = (bf16[512,256]{1,0:T(8,128)(2,1)}, bf16[512,256]{1,0:T(8,128)(2,1)S(1)}, u32[]{:S(2)}, u32[]{:S(2)}) collective-permute-start(bf16[512,256]{1,0:T(8,128)(2,1)} %get-tuple-element.63), channel_id=1, source_target_pairs={{0,32},{32,64},{64,96},{96,0},{1,33},{33,65},{65,97},{97,1},{2,34}... | collective-permute-start | bytes 786440 | tf_op jit(solution)/shard_map/ppermute | solution.py:255
  95.9 12.7 %all-to-all-start.2 = ((bf16[8,64,256]{2,1,0:T(8,128)(2,1)}), bf16[8,64,256]{2,1,0:T(8,128)(2,1)S(1)}, u32[]{:S(2)}, u32[]{:S(2)}) async-start(bf16[8,64,256]{2,1,0:T(8,128)(2,1)} %bitcast.17), calls=%async_computation.2 | async-start | bytes 524288 | tf_op jit(solution)/shard_map/all_to_all | solution.py:288
  108.6 14.1 %all-to-all-start.3 = ((bf16[8,64,256]{2,1,0:T(8,128)(2,1)}), bf16[8,64,256]{2,1,0:T(8,128)(2,1)S(1)}, u32[]{:S(2)}, u32[]{:S(2)}) async-start(bf16[8,64,256]{2,1,0:T(8,128)(2,1)} %bitcast.16), calls=%async_computation.3 | async-start | bytes 524288 | tf_op jit(solution)/shard_map/all_to_all | solution.py:288
  113.6 9.1 %collective-permute-start.22 = (bf16[64,1024]{1,0:T(8,128)(2,1)S(1)}, bf16[64,1024]{1,0:T(8,128)(2,1)S(1)}, u32[]{:S(2)}, u32[]{:S(2)}) collective-permute-start(bf16[64,1024]{1,0:T(8,128)(2,1)S(1)} %bitcast.72), channel_id=1, source_target_pairs={{0,24},{8,0},{16,8},{24,16},{1,25},{9,1},{17,9},{25,17},{2,26},{10... | collective-permute-start | bytes 393224 | tf_op jit(solution)/shard_map/ppermute | solution.py:255
  115.7 6.9 %collective-permute-start.21 = (bf16[64,1024]{1,0:T(8,128)(2,1)S(1)}, bf16[64,1024]{1,0:T(8,128)(2,1)S(1)}, u32[]{:S(2)}, u32[]{:S(2)}) collective-permute-start(bf16[64,1024]{1,0:T(8,128)(2,1)S(1)} %bitcast.73), channel_id=1, source_target_pairs={{0,16},{8,24},{16,0},{24,8},{1,17},{9,25},{17,1},{25,9},{2,18},{10... | collective-permute-start | bytes 393224 | tf_op jit(solution)/shard_map/ppermute | solution.py:255
  116.9 5.7 %collective-permute-start.20 = (bf16[64,1024]{1,0:T(8,128)(2,1)S(1)}, bf16[64,1024]{1,0:T(8,128)(2,1)S(1)}, u32[]{:S(2)}, u32[]{:S(2)}) collective-permute-start(bf16[64,1024]{1,0:T(8,128)(2,1)S(1)} %bitcast.74), channel_id=1, source_target_pairs={{0,8},{8,16},{16,24},{24,0},{1,9},{9,17},{17,25},{25,1},{2,10},{10... | collective-permute-start | bytes 393224 | tf_op jit(solution)/shard_map/ppermute | solution.py:255
  122.8 14.5 %collective-permute-start.25 = (bf16[64,1024]{1,0:T(8,128)(2,1)S(1)}, bf16[64,1024]{1,0:T(8,128)(2,1)S(1)}, u32[]{:S(2)}, u32[]{:S(2)}) collective-permute-start(bf16[64,1024]{1,0:T(8,128)(2,1)S(1)} %bitcast.77), channel_id=1, source_target_pairs={{0,24},{8,0},{16,8},{24,16},{1,25},{9,1},{17,9},{25,17},{2,26},{10... | collective-permute-start | bytes 393224 | tf_op jit(solution)/shard_map/ppermute | solution.py:255
  125.5 11.7 %collective-permute-start.24 = (bf16[64,1024]{1,0:T(8,128)(2,1)S(1)}, bf16[64,1024]{1,0:T(8,128)(2,1)S(1)}, u32[]{:S(2)}, u32[]{:S(2)}) collective-permute-start(bf16[64,1024]{1,0:T(8,128)(2,1)S(1)} %bitcast.78), channel_id=1, source_target_pairs={{0,16},{8,24},{16,0},{24,8},{1,17},{9,25},{17,1},{25,9},{2,18},{10... | collective-permute-start | bytes 393224 | tf_op jit(solution)/shard_map/ppermute | solution.py:255
  126.1 11.2 %collective-permute-start.23 = (bf16[64,1024]{1,0:T(8,128)(2,1)S(1)}, bf16[64,1024]{1,0:T(8,128)(2,1)S(1)}, u32[]{:S(2)}, u32[]{:S(2)}) collective-permute-start(bf16[64,1024]{1,0:T(8,128)(2,1)S(1)} %bitcast.79), channel_id=1, source_target_pairs={{0,8},{8,16},{16,24},{24,0},{1,9},{9,17},{17,25},{25,1},{2,10},{10... | collective-permute-start | bytes 393224 | tf_op jit(solution)/shard_map/ppermute | solution.py:255
  126.2 15.9 %collective-permute-start.27 = (bf16[64,1024]{1,0:T(8,128)(2,1)S(1)}, bf16[64,1024]{1,0:T(8,128)(2,1)S(1)}, u32[]{:S(2)}, u32[]{:S(2)}) collective-permute-start(bf16[64,1024]{1,0:T(8,128)(2,1)S(1)} %select_select_fusion), channel_id=1, source_target_pairs={{0,4},{4,0},{1,5},{5,1},{2,6},{6,2},{3,7},{7,3},{8,12},{12,8},{9,1... | collective-permute-start | bytes 393224 | tf_op jit(solution)/shard_map/ppermute | solution.py:255
  137.3 5.8 %collective-permute-start.26 = (bf16[64,1024]{1,0:T(8,128)(2,1)S(1)}, bf16[64,1024]{1,0:T(8,128)(2,1)S(1)}, u32[]{:S(2)}, u32[]{:S(2)}) collective-permute-start(bf16[64,1024]{1,0:T(8,128)(2,1)S(1)} %select_select_fusion.1), channel_id=1, source_target_pairs={{0,4},{4,0},{1,5},{5,1},{2,6},{6,2},{3,7},{7,3},{8,12},{12,8},{9,1... | collective-permute-start | bytes 393224 | tf_op jit(solution)/shard_map/ppermute | solution.py:255
